TPU v7x, 128 devices: a whole 4x4x4 slice. The times are simulated.
128 devices in a mesh: row: 8 (over z, x_hi), col: 16 (over y, x_lo, core).
Axes of the slice: x: 4 (x_hi: 2, x_lo: 2; x = x_hi * 2 + x_lo), y: 4, z: 4, core: 2. Of those that a mesh axis runs over, the one named last changes fastest.
Arguments:
- fine_in: bfloat16 [256, 2048, 128], P('row', 'col'), may hold values from -6 to 6
- coarse: bfloat16 [64, 32, 128], P('row'), may hold values from -6 to 6
- block_map: int32 [8, 16, 4], P('row', 'col'), may hold values from 0 to 63, as said below
- interp: bfloat16 [4, 128, 256, 2048], P(None, None, 'row', 'col'), may hold values from -0.25 to 0.25
- lift_weight: bfloat16 [32, 128], replicated, may hold values from -1 to 1
- conv_first: bfloat16 [3, 3, 128, 128], replicated, may hold values from -0.1875 to 0.1875
- conv_second: bfloat16 [3, 3, 128, 128], replicated, may hold values from -0.1875 to 0.1875
- cotangent: bfloat16 [256, 2048, 128], P('row', 'col'), may hold values from -6 to 6
Outputs:
- output: bfloat16 [256, 2048, 128], P('row', 'col')
- grad_fine: bfloat16 [256, 2048, 128], P('row', 'col')
- grad_coarse: float32 [64, 32, 128], P('row')
- grad_first: float32 [3, 3, 128, 128], replicated
- grad_second: float32 [3, 3, 128, 128], replicated
- grad_lift: float32 [32, 128], replicated
Inputs may be any that keep to these rules, and one draw needn't show every extreme that they name: `block_map`: every block named by tile (i, j) lies in rows i - 1, i or i + 1 of the blocks' rows of 8: from (i - 1) * 8 up to (i + 2) * 8 - 1, within the grid of blocks; each tile with i > 0 names at least one block of row i - 1 (it may name several) and each with i + 1 < 8 at least one of row i + 1.
All inputs are finite; a program needn't handle non-finite values.
Results may differ from a plain program's by a relative error of at most 0.009.
Values may be sent and summed in bfloat16 or wider, within the bound.
A program may use at most 128 MiB of HBM per device.

v0:
```python
import jax
import jax.numpy as jnp
from jax import lax
from jax.sharding import PartitionSpec as P


def extended(cells, sides, width):
    for axis, dim in sides:
        count = lax.axis_size(axis)
        ends = count - 1
        head = lax.slice_in_dim(cells, 0, width, axis=dim)
        tail = lax.slice_in_dim(cells, cells.shape[dim] - width, cells.shape[dim], axis=dim)
        cells = jnp.concatenate(
            [
                lax.ppermute(tail, axis, [(i, (i + 1) % count) for i in range(ends)]),
                cells,
                lax.ppermute(head, axis, [((i + 1) % count, i) for i in range(ends)]),
            ],
            axis=dim,
        )
    return cells


def passed_along(block, axis, distance):
    devices = range(lax.axis_size(axis))
    route = [(i - distance, i) for i in devices if i - distance in devices]
    return lax.ppermute(block, axis, route)


def widen(field):
    return extended(field, (("row", 0), ("col", 1)), 1)


def conv_taps(padded, kernel, rows, cols):
    total = jnp.zeros((rows * cols, kernel.shape[3]), jnp.float32)
    for shift_row in range(3):
        for shift_col in range(3):
            piece = padded[shift_row : shift_row + rows, shift_col : shift_col + cols].reshape(
                rows * cols, -1
            )
            total = total + jnp.dot(
                piece, kernel[shift_row, shift_col], preferred_element_type=jnp.float32
            )
    return total


def kernel_grad(padded, grad_flat, rows, cols):
    taps_list = []
    for shift_row in range(3):
        for shift_col in range(3):
            piece = padded[shift_row : shift_row + rows, shift_col : shift_col + cols].reshape(
                rows * cols, -1
            )
            taps_list.append(
                lax.dot_general(
                    piece, grad_flat, (((0,), (0,)), ((), ())), preferred_element_type=jnp.float32
                )
            )
    return jnp.stack(taps_list).reshape(3, 3, taps_list[0].shape[0], taps_list[0].shape[1])


def flipped(kernel):
    return jnp.transpose(jnp.flip(kernel, (0, 1)), (0, 1, 3, 2))


def body(fine_in, coarse, block_map, interp, lift_weight, conv_first, conv_second, cotangent):
    height, width, chans = fine_in.shape
    cells = height * width
    per_row = coarse.shape[0]
    slot_count = interp.shape[0]
    divisor = float(width * lax.axis_size("row"))
    weights = interp.reshape(slot_count, interp.shape[1], cells)
    picks = block_map.reshape(-1)
    window = extended(coarse, (("row", 0),), per_row)
    local_ids = picks - (lax.axis_index("row") - 1) * per_row
    upsum = jnp.zeros((coarse.shape[1], cells), jnp.float32)
    for slot in range(slot_count):
        block = lax.dynamic_index_in_dim(window, local_ids[slot], 0, keepdims=False)
        upsum = upsum + jnp.dot(block, weights[slot], preferred_element_type=jnp.float32)
    upward = upsum.astype(jnp.bfloat16)
    lifted = lax.dot_general(
        upward, lift_weight, (((0,), (0,)), ((), ())), preferred_element_type=jnp.float32
    )
    stem = (fine_in.reshape(cells, chans).astype(jnp.float32) + lifted).astype(jnp.bfloat16)
    stem_pad = widen(stem.reshape(height, width, chans))
    first_pre = conv_taps(stem_pad, conv_first, height, width)
    first_act = jax.nn.silu(first_pre).astype(jnp.bfloat16)
    act_pad = widen(first_act.reshape(height, width, chans))
    output = (stem.astype(jnp.float32) + conv_taps(act_pad, conv_second, height, width)).astype(
        jnp.bfloat16
    )
    cot_flat = cotangent.reshape(cells, chans)
    grad_act = conv_taps(widen(cotangent), flipped(conv_second), height, width)
    sigma = jax.nn.sigmoid(first_pre)
    grad_pre = (grad_act * (sigma * (1.0 + first_pre * (1.0 - sigma)))).astype(jnp.bfloat16)
    second_local = kernel_grad(act_pad, cot_flat, height, width)
    pre_pad = widen(grad_pre.reshape(height, width, chans))
    grad_fine = (
        cot_flat.astype(jnp.float32) + conv_taps(pre_pad, flipped(conv_first), height, width)
    ).astype(jnp.bfloat16)
    first_local = kernel_grad(stem_pad, grad_pre, height, width)
    lift_local = jnp.dot(upward, grad_fine, preferred_element_type=jnp.float32)
    grad_up = lax.dot_general(
        lift_weight, grad_fine, (((1,), (1,)), ((), ())), preferred_element_type=jnp.float32
    ).astype(jnp.bfloat16)
    window_count = window.shape[0]
    positions = jnp.arange(window_count, dtype=jnp.int32)
    window_grad = jnp.zeros((window_count, coarse.shape[1], coarse.shape[2]), jnp.float32)
    for slot in range(slot_count):
        block_grad = lax.dot_general(
            grad_up, weights[slot], (((1,), (1,)), ((), ())), preferred_element_type=jnp.float32
        )
        window_grad = window_grad + jnp.where(
            (positions == local_ids[slot])[:, None, None], block_grad[None], 0.0
        )
    from_below = passed_along(window_grad[:per_row].astype(jnp.bfloat16), "row", -1).astype(
        jnp.float32
    )
    from_above = passed_along(window_grad[2 * per_row :].astype(jnp.bfloat16), "row", 1).astype(
        jnp.float32
    )
    owned = window_grad[per_row : 2 * per_row] + from_below + from_above
    grad_coarse = lax.psum(owned, "col")
    first_total, second_total, lift_total = lax.psum(
        (first_local, second_local, lift_local), ("row", "col")
    )
    return (
        output.reshape(height, width, chans),
        grad_fine.reshape(height, width, chans),
        grad_coarse,
        first_total / divisor,
        second_total / divisor,
        lift_total / divisor,
    )


def solution(mesh):
    return jax.shard_map(
        body,
        mesh=mesh,
        in_specs=(
            P("row", "col", None),
            P("row", None, None),
            P("row", "col", None),
            P(None, None, "row", "col"),
            P(),
            P(),
            P(),
            P("row", "col", None),
        ),
        out_specs=(
            P("row", "col", None),
            P("row", "col", None),
            P("row", None, None),
            P(),
            P(),
            P(),
        ),
        check_vma=False,
    )
```

profile of v0, /device:TPU:1, one launch (start us, length us, event | category | flops | bytes accessed | tf_op | source)
XLA Modules:
  0.0 477.7 jit_solution(14109661240718563642)
XLA Ops:
  7.2 6.1 %collective-permute-start = (bf16[8,32,128]{2,1,0:T(8,128)(2,1)}, bf16[8,32,128]{2,1,0:T(8,128)(2,1)}, u32[]{:S(2)}, u32[]{:S(2)}) collective-permute-start(bf16[8,32,128]{2,1,0:T(8,128)(2,1)} %param.9), channel_id=1, source_target_pairs={{0,16},{16,32},{32,48},{48,64},{64,80},{80,96},{96,112},{1,17},{17... | collective-permute-start | bytes 196616 | tf_op jit(solution)/shard_map/ppermute | solution.py:15
  13.3 1.3 collective-permute-start.1
  14.6 1.4 fusion.140
  16.0 5.5 %collective-permute-start.10 = (bf16[1,128,128]{2,1,0:T(8,128)(2,1)}, bf16[1,128,128]{2,1,0:T(8,128)(2,1)S(1)}, u32[]{:S(2)}, u32[]{:S(2)}) collective-permute-start(bf16[1,128,128]{2,1,0:T(8,128)(2,1)} %get-tuple-element.61), channel_id=1, source_target_pairs={{0,16},{16,32},{32,48},{48,64},{64,80},{80,96},{96,112},{1,17},{17... | collective-permute-start | bytes 98312 | tf_op jit(solution)/shard_map/ppermute | solution.py:15
  21.5 1.3 collective-permute-start.11
  24.1 4.5 fusion.131
  29.6 1.3 iota_compare_fusion
  30.9 1.9 iota_compare_fusion.2
  41.5 3.6 collective-permute-start.12
  45.1 1.9 collective-permute-start.13
  47.9 2.3 collective-permute-done.13
  50.2 3.0 pad_maximum_fusion.8
  59.9 6.4 %collective-permute-start.2 = (bf16[1,128,128]{2,1,0:T(8,128)(2,1)S(1)}, bf16[1,128,128]{2,1,0:T(8,128)(2,1)S(1)}, u32[]{:S(2)}, u32[]{:S(2)}) collective-permute-start(bf16[1,128,128]{2,1,0:T(8,128)(2,1)S(1)} %get-tuple-element.68), channel_id=1, source_target_pairs={{0,16},{16,32},{32,48},{48,64},{64,80},{80,96},{96,112},{1,17},{17... | collective-permute-start | bytes 98312 | tf_op jit(solution)/shard_map/ppermute | solution.py:15
  66.3 1.3 collective-permute-start.3
  67.6 1.2 fusion.68
  68.8 3.8 collective-permute-done.3
  72.6 3.2 collective-permute-start.4
  75.8 2.4 collective-permute-start.5
  78.8 2.1 collective-permute-done.5
  87.2 6.6 %collective-permute-start.6 = (bf16[1,128,128]{2,1,0:T(8,128)(2,1)S(1)}, bf16[1,128,128]{2,1,0:T(8,128)(2,1)S(1)}, u32[]{:S(2)}, u32[]{:S(2)}) collective-permute-start(bf16[1,128,128]{2,1,0:T(8,128)(2,1)S(1)} %get-tuple-element.64), channel_id=1, source_target_pairs={{0,16},{16,32},{32,48},{48,64},{64,80},{80,96},{96,112},{1,17},{17... | collective-permute-start | bytes 98312 | tf_op jit(solution)/shard_map/ppermute | solution.py:15
  93.9 1.3 collective-permute-start.7
  95.2 1.9 fusion.9
  102.9 2.3 copy.37
  105.2 5.5 %collective-permute-start.14 = (bf16[1,128,128]{2,1,0:T(8,128)(2,1)}, bf16[1,128,128]{2,1,0:T(8,128)(2,1)S(1)}, u32[]{:S(2)}, u32[]{:S(2)}) collective-permute-start(bf16[1,128,128]{2,1,0:T(8,128)(2,1)} %get-tuple-element.55), channel_id=1, source_target_pairs={{0,16},{16,32},{32,48},{48,64},{64,80},{80,96},{96,112},{1,17},{17... | collective-permute-start | bytes 98312 | tf_op jit(solution)/shard_map/ppermute | solution.py:15
  110.7 1.3 collective-permute-start.15
  113.0 1.4 pad_maximum_fusion.3
  114.4 1.8 fusion.139
  116.2 2.3 copy.39
  118.5 2.1 collective-permute-start.8
  120.7 2.3 copy.45
  123.0 2.7 collective-permute-start.9
  126.4 3.2 collective-permute-start.16
  129.6 1.9 collective-permute-start.17
  132.6 2.6 fusion.67
  135.2 1.4 pad_maximum_fusion.10
  136.7 2.3 copy.44
  139.0 2.3 copy.53
  141.3 1.4 maximum_maximum_fusion.2
  152.7 2.1 copy.40
  154.8 2.1 copy.46
  157.0 3.5 pad_maximum_fusion
  160.9 2.0 fusion.133
  163.4 2.7 fusion.132
  171.6 1.3 collective-permute-start.18
  172.8 7.4 %collective-permute-start.19 = (bf16[8,32,128]{2,1,0:T(8,128)(2,1)S(1)}, bf16[8,32,128]{2,1,0:T(8,128)(2,1)}, u32[]{:S(2)}, u32[]{:S(2)}) collective-permute-start(bf16[8,32,128]{2,1,0:T(8,128)(2,1)S(1)} %get-tuple-element.71), channel_id=1, source_target_pairs={{0,16},{16,32},{32,48},{48,64},{64,80},{80,96},{96,112},{1,17},{17... | collective-permute-start | bytes 196616 | tf_op jit(solution)/shard_map/ppermute | solution.py:27
  180.9 2.6 fusion.79
  183.5 1.3 copy.47
  184.8 1.6 copy.48
  186.5 2.1 convolution_add_fusion.20
  189.8 1.3 convolution_add_fusion.18
  191.1 2.5 convolution_add_fusion.17
  193.6 1.7 copy.49
  195.3 1.3 copy.50
  196.6 1.6 copy.54
  198.3 2.1 convolution_add_fusion.16
  200.5 1.3 convolution_add_fusion.15
  202.9 2.3 fusion.8
  205.5 70.8 %psum.31 = f32[32,128]{1,0:T(8,128)S(1)} all-reduce(f32[32,128]{1,0:T(8,128)S(1)} %fusion.143), channel_id=1, replica_groups=mesh['row'=8,'col'=16] {'row','col'}, use_global_device_ids=true, to_apply=%region_3.4 | all-reduce | flops 4096 | bytes 32768 | tf_op jit(solution)/shard_map/psum | solution.py:124
  276.9 1.6 fusion.65
  278.5 73.6 %all-reduce.6.cloned.1.call-done = (f32[3,3,128,128]{3,2,1,0:T(8,128)}, f32[3,3,128,128]{3,2,1,0:T(8,128)}) async-done(((f32[3,3,128,128]{3,2,1,0:T(8,128)}, f32[3,3,128,128]{3,2,1,0:T(8,128)}), (f32[3,3,128,128]{3,2,1,0:T(8,128)}, f32[3,3,128,128]{3,2,1,0:T(8,128)})) %all-reduce.6.cloned.1.call-update) | async-done | bytes 1179664 | tf_op jit(solution)/shard_map/psum | solution.py:124
  352.2 1.9 broadcast_multiply_fusion
  354.1 1.9 broadcast_multiply_fusion.1
  356.0 113.1 %all-reduce.4.cloned.1.call-done = f32[8,32,128]{2,1,0:T(8,128)} async-done(((f32[8,32,128]{2,1,0:T(8,128)}), f32[8,32,128]{2,1,0:T(8,128)}) %all-reduce.4.cloned.1.call-update) | async-done | bytes 131088 | tf_op jit(solution)/shard_map/psum | solution.py:123
  469.1 1.6 copy.114
  (178 shorter events, 45.7 us)
Async XLA Ops:
  7.2 52.0 %copy-start = (bf16[32,128]{1,0:T(8,128)(2,1)S(1)}, bf16[32,128]{1,0:T(8,128)(2,1)}, u32[]{:S(2)}) copy-start(bf16[32,128]{1,0:T(8,128)(2,1)} %param.12) | copy-start | bytes 24580
  7.2 345.0 %all-reduce.6.cloned.1.call-start = ((), (), s32[]{:S(2)}) async-start(), calls=%async_computation.1 | async-start | bytes 2359296 | tf_op jit(solution)/shard_map/psum | solution.py:124
  7.2 48.2 %collective-permute-start = (bf16[8,32,128]{2,1,0:T(8,128)(2,1)}, bf16[8,32,128]{2,1,0:T(8,128)(2,1)}, u32[]{:S(2)}, u32[]{:S(2)}) collective-permute-start(bf16[8,32,128]{2,1,0:T(8,128)(2,1)} %param.9), channel_id=1, source_target_pairs={{0,16},{16,32},{32,48},{48,64},{64,80},{80,96},{96,112},{1,17},{17... | collective-permute-start | bytes 196616 | tf_op jit(solution)/shard_map/ppermute | solution.py:15
  13.3 43.0 %collective-permute-start.1 = (bf16[8,32,128]{2,1,0:T(8,128)(2,1)}, bf16[8,32,128]{2,1,0:T(8,128)(2,1)}, u32[]{:S(2)}, u32[]{:S(2)}) collective-permute-start(bf16[8,32,128]{2,1,0:T(8,128)(2,1)} %param.9), channel_id=1, source_target_pairs={{16,0},{32,16},{48,32},{64,48},{80,64},{96,80},{112,96},{17,1},{33... | collective-permute-start | bytes 196616 | tf_op jit(solution)/shard_map/ppermute | solution.py:17
  16.0 24.7 %collective-permute-start.10 = (bf16[1,128,128]{2,1,0:T(8,128)(2,1)}, bf16[1,128,128]{2,1,0:T(8,128)(2,1)S(1)}, u32[]{:S(2)}, u32[]{:S(2)}) collective-permute-start(bf16[1,128,128]{2,1,0:T(8,128)(2,1)} %get-tuple-element.61), channel_id=1, source_target_pairs={{0,16},{16,32},{32,48},{48,64},{64,80},{80,96},{96,112},{1,17},{17... | collective-permute-start | bytes 98312 | tf_op jit(solution)/shard_map/ppermute | solution.py:15
  21.5 19.2 %collective-permute-start.11 = (bf16[1,128,128]{2,1,0:T(8,128)(2,1)S(1)}, bf16[1,128,128]{2,1,0:T(8,128)(2,1)S(1)}, u32[]{:S(2)}, u32[]{:S(2)}) collective-permute-start(bf16[1,128,128]{2,1,0:T(8,128)(2,1)S(1)} %get-tuple-element.60), channel_id=1, source_target_pairs={{16,0},{32,16},{48,32},{64,48},{80,64},{96,80},{112,96},{17,1},{33... | collective-permute-start | bytes 98312 | tf_op jit(solution)/shard_map/ppermute | solution.py:17
  24.1 4.6 copy-start.26
  24.1 4.6 copy-start.28
  24.1 16.6 %copy-start.1 = (bf16[32,128,128]{2,1,0:T(8,128)(2,1)S(1)}, bf16[32,128,128]{2,1,0:T(8,128)(2,1)}, u32[]{:S(2)}) copy-start(bf16[32,128,128]{2,1,0:T(8,128)(2,1)} %param.15) | copy-start | bytes 3145732
  28.7 29.5 %copy-start.11 = (bf16[1,128,32,128]{3,2,1,0:T(8,128)(2,1)}, bf16[1,128,32,128]{3,2,1,0:T(8,128)(2,1)S(1)}, u32[]{:S(2)}) copy-start(bf16[1,128,32,128]{3,2,1,0:T(8,128)(2,1)S(1)} %get-tuple-element.10) | copy-start | bytes 3145732
  28.7 29.9 %copy-start.9 = (bf16[1,128,32,128]{3,2,1,0:T(8,128)(2,1)}, bf16[1,128,32,128]{3,2,1,0:T(8,128)(2,1)S(1)}, u32[]{:S(2)}) copy-start(bf16[1,128,32,128]{3,2,1,0:T(8,128)(2,1)S(1)} %get-tuple-element.8) | copy-start | bytes 3145732
  28.7 26.2 %copy-start.30 = (bf16[3,3,128,128]{2,3,1,0:T(8,128)(2,1)}, bf16[3,3,128,128]{2,3,1,0:T(8,128)(2,1)S(1)}, u32[]{:S(2)}) copy-start(bf16[3,3,128,128]{2,3,1,0:T(8,128)(2,1)S(1)} %reverse_bitcast_fusion.1) | copy-start | bytes 884740
  41.5 6.4 %collective-permute-start.12 = (bf16[34,1,128]{2,1,0:T(2,128)(2,1)S(1)}, bf16[34,1,128]{2,1,0:T(2,128)(2,1)S(1)}, u32[]{:S(2)}, u32[]{:S(2)}) collective-permute-start(bf16[34,1,128]{2,1,0:T(2,128)(2,1)S(1)} %get-tuple-element.43), channel_id=1, source_target_pairs={{0,1},{1,2},{2,3},{3,4},{4,5},{5,6},{6,7},{7,8},{8,9},{9,10},{10,1... | collective-permute-start | bytes 26120 | tf_op jit(solution)/shard_map/ppermute | solution.py:15
  45.1 5.1 %collective-permute-start.13 = (bf16[34,1,128]{2,1,0:T(2,128)(2,1)S(1)}, bf16[34,1,128]{2,1,0:T(2,128)(2,1)S(1)}, u32[]{:S(2)}, u32[]{:S(2)}) collective-permute-start(bf16[34,1,128]{2,1,0:T(2,128)(2,1)S(1)} %get-tuple-element.44), channel_id=1, source_target_pairs={{1,0},{2,1},{3,2},{4,3},{5,4},{6,5},{7,6},{8,7},{9,8},{10,9},{11,1... | collective-permute-start | bytes 26120 | tf_op jit(solution)/shard_map/ppermute | solution.py:17
  54.9 1.4 copy-start.34
  55.0 2.3 copy-start.13
  55.4 2.3 copy-start.15
  58.2 1.2 copy-start.31
  59.9 8.9 %collective-permute-start.2 = (bf16[1,128,128]{2,1,0:T(8,128)(2,1)S(1)}, bf16[1,128,128]{2,1,0:T(8,128)(2,1)S(1)}, u32[]{:S(2)}, u32[]{:S(2)}) collective-permute-start(bf16[1,128,128]{2,1,0:T(8,128)(2,1)S(1)} %get-tuple-element.68), channel_id=1, source_target_pairs={{0,16},{16,32},{32,48},{48,64},{64,80},{80,96},{96,112},{1,17},{17... | collective-permute-start | bytes 98312 | tf_op jit(solution)/shard_map/ppermute | solution.py:15
  66.3 6.3 %collective-permute-start.3 = (bf16[1,128,128]{2,1,0:T(8,128)(2,1)S(1)}, bf16[1,128,128]{2,1,0:T(8,128)(2,1)S(1)}, u32[]{:S(2)}, u32[]{:S(2)}) collective-permute-start(bf16[1,128,128]{2,1,0:T(8,128)(2,1)S(1)} %get-tuple-element.69), channel_id=1, source_target_pairs={{16,0},{32,16},{48,32},{64,48},{80,64},{96,80},{112,96},{17,1},{33... | collective-permute-start | bytes 98312 | tf_op jit(solution)/shard_map/ppermute | solution.py:17
  72.6 5.8 %copy-start.29 = (bf16[3,3,128,128]{3,2,1,0:T(8,128)(2,1)S(1)}, bf16[3,3,128,128]{3,2,1,0:T(8,128)(2,1)}, u32[]{:S(2)}) copy-start(bf16[3,3,128,128]{3,2,1,0:T(8,128)(2,1)} %param.13) | copy-start | bytes 884740
  72.6 6.2 %collective-permute-start.4 = (bf16[34,1,128]{2,1,0:T(2,128)(2,1)S(1)}, bf16[34,1,128]{2,1,0:T(2,128)(2,1)S(1)}, u32[]{:S(2)}, u32[]{:S(2)}) collective-permute-start(bf16[34,1,128]{2,1,0:T(2,128)(2,1)S(1)} %get-tuple-element.51), channel_id=1, source_target_pairs={{0,1},{1,2},{2,3},{3,4},{4,5},{5,6},{6,7},{7,8},{8,9},{9,10},{10,1... | collective-permute-start | bytes 26120 | tf_op jit(solution)/shard_map/ppermute | solution.py:15
  75.8 5.1 %collective-permute-start.5 = (bf16[34,1,128]{2,1,0:T(2,128)(2,1)S(1)}, bf16[34,1,128]{2,1,0:T(2,128)(2,1)S(1)}, u32[]{:S(2)}, u32[]{:S(2)}) collective-permute-start(bf16[34,1,128]{2,1,0:T(2,128)(2,1)S(1)} %get-tuple-element.52), channel_id=1, source_target_pairs={{1,0},{2,1},{3,2},{4,3},{5,4},{6,5},{7,6},{8,7},{9,8},{10,9},{11,1... | collective-permute-start | bytes 26120 | tf_op jit(solution)/shard_map/ppermute | solution.py:17
  86.5 10.5 %copy-start.4 = (bf16[4096,128]{1,0:T(8,128)(2,1)}, bf16[4096,128]{1,0:T(8,128)(2,1)S(1)}, u32[]{:S(2)}) copy-start(bf16[4096,128]{1,0:T(8,128)(2,1)S(1)} %get-tuple-element.78) | copy-start | bytes 3145732
  87.2 24.8 %collective-permute-start.6 = (bf16[1,128,128]{2,1,0:T(8,128)(2,1)S(1)}, bf16[1,128,128]{2,1,0:T(8,128)(2,1)S(1)}, u32[]{:S(2)}, u32[]{:S(2)}) collective-permute-start(bf16[1,128,128]{2,1,0:T(8,128)(2,1)S(1)} %get-tuple-element.64), channel_id=1, source_target_pairs={{0,16},{16,32},{32,48},{48,64},{64,80},{80,96},{96,112},{1,17},{17... | collective-permute-start | bytes 98312 | tf_op jit(solution)/shard_map/ppermute | solution.py:15
  93.9 18.3 %collective-permute-start.7 = (bf16[1,128,128]{2,1,0:T(8,128)(2,1)}, bf16[1,128,128]{2,1,0:T(8,128)(2,1)}, u32[]{:S(2)}, u32[]{:S(2)}) collective-permute-start(bf16[1,128,128]{2,1,0:T(8,128)(2,1)} %get-tuple-element.65), channel_id=1, source_target_pairs={{16,0},{32,16},{48,32},{64,48},{80,64},{96,80},{112,96},{17,1},{33... | collective-permute-start | bytes 98312 | tf_op jit(solution)/shard_map/ppermute | solution.py:17
  101.5 0.8 copy-start.32
  105.2 20.5 %collective-permute-start.14 = (bf16[1,128,128]{2,1,0:T(8,128)(2,1)}, bf16[1,128,128]{2,1,0:T(8,128)(2,1)S(1)}, u32[]{:S(2)}, u32[]{:S(2)}) collective-permute-start(bf16[1,128,128]{2,1,0:T(8,128)(2,1)} %get-tuple-element.55), channel_id=1, source_target_pairs={{0,16},{16,32},{32,48},{48,64},{64,80},{80,96},{96,112},{1,17},{17... | collective-permute-start | bytes 98312 | tf_op jit(solution)/shard_map/ppermute | solution.py:15
  110.7 15.0 %collective-permute-start.15 = (bf16[1,128,128]{2,1,0:T(8,128)(2,1)}, bf16[1,128,128]{2,1,0:T(8,128)(2,1)S(1)}, u32[]{:S(2)}, u32[]{:S(2)}) collective-permute-start(bf16[1,128,128]{2,1,0:T(8,128)(2,1)} %get-tuple-element.56), channel_id=1, source_target_pairs={{16,0},{32,16},{48,32},{64,48},{80,64},{96,80},{112,96},{17,1},{33... | collective-permute-start | bytes 98312 | tf_op jit(solution)/shard_map/ppermute | solution.py:17
  118.5 34.1 %collective-permute-start.8 = (bf16[34,1,128]{2,0,1:T(8,128)(2,1)}, bf16[34,1,128]{2,0,1:T(8,128)(2,1)}, u32[]{:S(2)}, u32[]{:S(2)}) collective-permute-start(bf16[34,1,128]{2,0,1:T(8,128)(2,1)} %copy.39), channel_id=1, source_target_pairs={{0,1},{1,2},{2,3},{3,4},{4,5},{5,6},{6,7},{7,8},{8,9},{9,10},{10,1... | collective-permute-start | bytes 26120 | tf_op jit(solution)/shard_map/ppermute | solution.py:15
  123.0 31.8 %collective-permute-start.9 = (bf16[34,1,128]{2,0,1:T(8,128)(2,1)}, bf16[34,1,128]{2,0,1:T(8,128)(2,1)}, u32[]{:S(2)}, u32[]{:S(2)}) collective-permute-start(bf16[34,1,128]{2,0,1:T(8,128)(2,1)} %copy.45), channel_id=1, source_target_pairs={{1,0},{2,1},{3,2},{4,3},{5,4},{6,5},{7,6},{8,7},{9,8},{10,9},{11,1... | collective-permute-start | bytes 26120 | tf_op jit(solution)/shard_map/ppermute | solution.py:17
  126.4 14.9 %collective-permute-start.16 = (bf16[34,1,128]{2,1,0:T(2,128)(2,1)}, bf16[34,1,128]{2,1,0:T(2,128)(2,1)}, u32[]{:S(2)}, u32[]{:S(2)}) collective-permute-start(bf16[34,1,128]{2,1,0:T(2,128)(2,1)} %get-tuple-element.38), channel_id=1, source_target_pairs={{0,1},{1,2},{2,3},{3,4},{4,5},{5,6},{6,7},{7,8},{8,9},{9,10},{10,1... | collective-permute-start | bytes 26120 | tf_op jit(solution)/shard_map/ppermute | solution.py:15
  129.6 11.7 %collective-permute-start.17 = (bf16[34,1,128]{2,1,0:T(2,128)(2,1)}, bf16[34,1,128]{2,1,0:T(2,128)(2,1)}, u32[]{:S(2)}, u32[]{:S(2)}) collective-permute-start(bf16[34,1,128]{2,1,0:T(2,128)(2,1)} %get-tuple-element.39), channel_id=1, source_target_pairs={{1,0},{2,1},{3,2},{4,3},{5,4},{6,5},{7,6},{8,7},{9,8},{10,9},{11,1... | collective-permute-start | bytes 26120 | tf_op jit(solution)/shard_map/ppermute | solution.py:17
  132.6 2.6 copy-start.2
  143.5 1.6 copy-start.17
  143.5 1.6 copy-start.27
  147.7 1.2 copy-start.18
  148.9 1.2 copy-start.10
  149.5 2.6 copy-start.7
  149.5 1.7 copy-start.16
  149.5 2.1 copy-start.14
  150.2 2.0 copy-start.12
  152.2 4.8 %copy-start.3 = (bf16[32,128,128]{1,2,0:T(8,128)(2,1)S(1)}, bf16[32,128,128]{1,2,0:T(8,128)(2,1)}, u32[]{:S(2)}) copy-start(bf16[32,128,128]{1,2,0:T(8,128)(2,1)} %copy.37) | copy-start | bytes 3145732
  166.1 1.2 copy-start.5
  168.9 1.1 copy-start.35
  168.9 1.1 copy-start.36
  169.3 10.9 %copy-start.24 = (bf16[32,128,128]{1,2,0:T(8,128)(2,1)S(1)}, bf16[32,128,128]{1,2,0:T(8,128)(2,1)}, u32[]{:S(2)}) copy-start(bf16[32,128,128]{1,2,0:T(8,128)(2,1)} %get-tuple-element.17) | copy-start | bytes 3145732
  169.9 10.3 %copy-start.33 = (f32[9,128,128]{2,1,0:T(8,128)}, f32[9,128,128]{2,1,0:T(8,128)S(1)}, u32[]{:S(2)}) copy-start(f32[9,128,128]{2,1,0:T(8,128)S(1)} %fusion.16) | copy-start | bytes 1769476
  171.6 105.4 %collective-permute-start.18 = (bf16[8,32,128]{2,1,0:T(8,128)(2,1)}, bf16[8,32,128]{2,1,0:T(8,128)(2,1)S(1)}, u32[]{:S(2)}, u32[]{:S(2)}) collective-permute-start(bf16[8,32,128]{2,1,0:T(8,128)(2,1)} %get-tuple-element.70), channel_id=1, source_target_pairs={{16,0},{32,16},{48,32},{64,48},{80,64},{96,80},{112,96},{17,1},{33... | collective-permute-start | bytes 196616 | tf_op jit(solution)/shard_map/ppermute | solution.py:27
  172.8 104.1 %collective-permute-start.19 = (bf16[8,32,128]{2,1,0:T(8,128)(2,1)S(1)}, bf16[8,32,128]{2,1,0:T(8,128)(2,1)}, u32[]{:S(2)}, u32[]{:S(2)}) collective-permute-start(bf16[8,32,128]{2,1,0:T(8,128)(2,1)S(1)} %get-tuple-element.71), channel_id=1, source_target_pairs={{0,16},{16,32},{32,48},{48,64},{64,80},{80,96},{96,112},{1,17},{17... | collective-permute-start | bytes 196616 | tf_op jit(solution)/shard_map/ppermute | solution.py:27
  180.9 2.6 copy-start.25
  183.5 3.0 copy-start.20
  186.5 2.1 copy-start.22
  189.8 1.3 copy-start.6
  193.6 1.7 copy-start.23
  198.2 270.9 %all-reduce.4.cloned.1.call-start = ((), (), s32[]{:S(2)}) async-start(), calls=%async_computation | async-start | bytes 262144 | tf_op jit(solution)/shard_map/psum | solution.py:123
  198.3 2.1 copy-start.21
  200.4 1.3 copy-start.19
  202.9 2.3 copy-start.8
Sparse Core Ops, SparseCore 0:
  198.4 153.7 all-reduce.5
  355.3 113.7 all-reduce.3
where the time goes:
time: 486 us; the launch traced here: 478 us
  waiting for transfers between devices  195 us (40%)
  blocking collectives  70.8 us (15%)
  starting transfers between devices  66.5 us (14%)
  local copies, waits for them, and re-layouts  50.8 us (10%)
  matrix products  46.5 us (10%)
  other arithmetic  24.9 us (5%)
  between operations  23.2 us (5%)
    psum x1, waiting for transfers between devices, body(): grad_coarse = lax.psum(owned, 'col')  113 us
    psum x1, waiting for transfers between devices, body(): lax.psum((first_local, second_local, lift_local), ('row', 'col'))  73.6 us
    psum x1, blocking collectives, body(): lax.psum((first_local, second_local, lift_local), ('row', 'col'))  70.8 us
    ppermute x9, starting transfers between devices, extended(): lax.ppermute(tail, axis, [(i, (i + 1) % count) for i in range(ends)])  42.3 us
    dot_general x36, matrix products, conv_taps(): jnp.dot(piece, kernel[shift_row, shift_col], preferred_element_type=jnp.f...  32.9 us
    slice x13, local copies, waits for them, and re-layouts, conv_taps(): padded[shift_row:shift_row + rows, shift_col:shift_col + cols]  20.3 us
    ppermute x9, starting transfers between devices, extended(): lax.ppermute(head, axis, [((i + 1) % count, i) for i in range(ends)])  15.4 us
    concatenate x8, other arithmetic, extended(): jnp.concatenate([lax.ppermute(tail, axis, [(i, (i + 1) % count) for i in...  11.9 us
  transfers between devices with their start and end apart: 22, of which 5 were waited for; matrix products, arithmetic and copies ran while one was open for 19% of the time, Pallas kernels for 0%

commit v1 on v0

v1 whole, which is shorter than its diff:
```python
import functools

import jax
import jax.numpy as jnp
from jax import lax
from jax.experimental import pallas as pl
from jax.experimental.pallas import tpu as pltpu
from jax.sharding import PartitionSpec as P

MESH = pl.DeviceIdType.MESH
BF = jnp.bfloat16
F32 = jnp.float32
PITCH = 144
CHUNK = 80


def rows_of(row, count=1, pitch=128):
    start = row * pitch
    if not isinstance(start, int):
        start = pl.multiple_of(start, pitch if pitch == 128 else 16)
    return pl.ds(start, count * pitch)


def pair_conv(x3, wp, first, pairs):
    parts = []
    for j in range(4):
        parts.append(
            jnp.concatenate([x3[rows_of(first + 2 * p + j), :] for p in range(pairs)], 0)
        )
    return jnp.dot(jnp.concatenate(parts, 1), wp[...], preferred_element_type=F32)


def side_conv(pad, wp):
    sides = []
    for base in (6, 135):
        sides.append(
            jnp.concatenate(
                [
                    pad[pl.ds(a * PITCH + base + e, 40, stride=PITCH), :].astype(BF)
                    for a in range(3)
                    for e in range(3)
                ],
                1,
            )
        )
    return jnp.dot(
        jnp.concatenate(sides, 0), wp[0:1152, 0:128], preferred_element_type=F32
    )


def shifted_row(pad, x3, row):
    start = row * PITCH + 8
    for e in range(3):
        x3[rows_of(row), e * 128 : (e + 1) * 128] = pad[pl.ds(start + e - 1, 128), :].astype(BF)


def gate(pre, grad):
    s = 0.5 * (1.0 + jnp.tanh(0.5 * pre))
    return pre * s, grad * (s * (1.0 + pre * (1.0 - s)))


def kernel(
    n_row,
    n_col,
    fine,
    coarse,
    ids,
    interp,
    lift,
    first,
    second,
    cot,
    out,
    grad_fine,
    grad_coarse,
    grad_first,
    grad_second,
    grad_lift,
    fine_v,
    interp_v,
    weights_it,
    window,
    lift_v,
    first_v,
    second_v,
    wp_first,
    wp_second,
    wp_first_f,
    wp_second_f,
    pad_cot,
    pad_stem,
    pad_act,
    pad_pre,
    x3_cot,
    x3_stem,
    x3_act,
    x3_pre,
    cot_z,
    pre_z,
    stem_v,
    grad_act,
    gf_v,
    out_v,
    mix,
    edge_send,
    land_row,
    land_col,
    land_corner,
    taps,
    local,
    land0,
    half,
    land1,
    land2,
    final,
    wide,
    coarse_wide,
    lift_wide,
    copy_sem,
    out_sem,
    coarse_send,
    coarse_recv,
    halo_send,
    halo_recv,
    s0_send,
    s0_recv,
    s1_send,
    s1_recv,
    s2_send,
    s2_recv,
    s3_send,
    s3_recv,
    s4_send,
    s4_recv,
):
    r = lax.axis_index("row")
    c = lax.axis_index("col")
    nq = n_col // 2
    q = lax.div(c, 2)
    h = lax.rem(c, 2)
    sibling = c + 1 - 2 * h
    own = h * nq + q
    up = lax.rem(r + n_row - 1, n_row)
    down = lax.rem(r + 1, n_row)
    left = lax.rem(c + n_col - 1, n_col)
    right = lax.rem(c + 1, n_col)
    q_peers = [lax.rem(q + d, nq) for d in range(1, nq)]
    r_peers = [lax.rem(r + d, n_row) for d in range(1, n_row)]

    around = [
        (up, c), (down, c), (r, left), (r, right),
        (up, left), (up, right), (down, left), (down, right),
    ]
    barrier = pltpu.get_barrier_semaphore()
    peers = (
        around
        + [(r, 2 * peer + h) for peer in q_peers]
        + [(peer, c) for peer in r_peers[1:-1]]
    )
    for peer in peers:
        pl.semaphore_signal(barrier, inc=1, device_id=peer, device_id_type=MESH)

    copies = [
        pltpu.make_async_copy(cot, cot_z.at[2:34], copy_sem.at[0]),
        pltpu.make_async_copy(coarse, window.at[8:16], copy_sem.at[1]),
        pltpu.make_async_copy(first, first_v, copy_sem.at[2]),
        pltpu.make_async_copy(second, second_v, copy_sem.at[3]),
        pltpu.make_async_copy(lift, lift_v, copy_sem.at[4]),
        pltpu.make_async_copy(interp, interp_v, copy_sem.at[5]),
        pltpu.make_async_copy(fine, fine_v, copy_sem.at[6]),
    ]
    for copy in copies:
        copy.start()

    def cot_rows(row):
        return cot_z[row].astype(F32)

    zero_row = jnp.zeros((2, 128, 128), BF)
    cot_z[0:2] = zero_row
    cot_z[34:36] = zero_row
    pre_z[0:2] = zero_row
    pre_z[34:36] = zero_row
    copies[0].wait()

    def cot_step(i, carry):
        pad_cot[pl.ds(pl.multiple_of(i * PITCH, 16) + 8, 128), :] = cot_rows(i)
        shifted_row(pad_cot, x3_cot, i)
        return carry

    lax.fori_loop(2, 34, cot_step, 0)

    def fill_edges(pad, which):
        for side, columns in enumerate(((0, 1), (126, 127))):
            for j, x in enumerate(columns):
                edge_send[which, side, j] = pad[
                    pl.ds(2 * PITCH + 8 + x, 32, stride=PITCH), :
                ].astype(BF)

    fill_edges(pad_cot, 0)
    pl.semaphore_wait(barrier, len(peers))

    coarse_copies = [
        pltpu.make_async_remote_copy(
            coarse, window.at[16:24], coarse_send.at[0], coarse_recv.at[0], (up, c), MESH
        ),
        pltpu.make_async_remote_copy(
            coarse, window.at[0:8], coarse_send.at[1], coarse_recv.at[1], (down, c), MESH
        ),
    ]
    for copy in coarse_copies:
        copy.start()

    def halo_copies(which, head, tail):
        def copy(k, src, dst, device):
            return pltpu.make_async_remote_copy(
                src, dst, halo_send.at[which, k], halo_recv.at[which, k], device, MESH
            )

        edges = edge_send.at[which]
        return [
            copy(0, head, land_row.at[which, 1], (up, c)),
            copy(1, tail, land_row.at[which, 0], (down, c)),
            copy(2, edges.at[0], land_col.at[which, 1], (r, left)),
            copy(3, edges.at[1], land_col.at[which, 0], (r, right)),
            copy(4, edges.at[0, :, 0:16], land_corner.at[which, 3], (up, left)),
            copy(5, edges.at[1, :, 0:16], land_corner.at[which, 2], (up, right)),
            copy(6, edges.at[0, :, 16:32], land_corner.at[which, 1], (down, left)),
            copy(7, edges.at[1, :, 16:32], land_corner.at[which, 0], (down, right)),
        ]

    cot_halos = halo_copies(0, cot_z.at[2:4], cot_z.at[32:34])
    for copy in cot_halos:
        copy.start()

    copies[2].wait()
    copies[3].wait()
    for wp in (wp_first, wp_second, wp_first_f, wp_second_f):
        wp[1152:1536, 0:128] = jnp.zeros((384, 128), BF)
        wp[0:384, 128:256] = jnp.zeros((384, 128), BF)
    for raw, wp, wp_f in ((first_v, wp_first, wp_first_f), (second_v, wp_second, wp_second_f)):
        for a in range(3):
            for e in range(3):
                tap = raw[a, e]
                turned = raw[2 - a, 2 - e].astype(F32).T.astype(BF)
                low = a * 384 + e * 128
                for target, value in ((wp, tap), (wp_f, turned)):
                    target[low : low + 128, 0:128] = value
                    target[low + 384 : low + 512, 128:256] = value

    copies[5].wait()

    def turn(i, carry):
        slot = lax.div(i, 4)
        block = lax.rem(i, 4)
        piece = jnp.swapaxes(interp_v[slot, pl.ds(block * 32, 32)], 0, 1)
        for y in range(32):
            weights_it[pl.ds(pl.multiple_of(i * 32, 32), 32), y * 128 : (y + 1) * 128] = piece[y]
        return carry

    lax.fori_loop(0, 16, turn, 0)

    copies[1].wait()
    copies[4].wait()
    copies[6].wait()
    for copy in coarse_copies:
        copy.wait()
    local_ids = [jnp.clip(ids[k] - (r - 1) * 8, 0, 23) for k in range(4)]
    picked = jnp.concatenate([window[local_ids[k]] for k in range(4)], 1)
    mix[...] = lax.dot_general(
        picked, lift_v[...], (((0,), (0,)), ((), ())), preferred_element_type=F32
    ).astype(BF)

    def stem_step(i, carry):
        lifted = lax.dot_general(
            weights_it[:, pl.ds(pl.multiple_of(i * 512, 512), 512)],
            mix[...],
            (((0,), (0,)), ((), ())),
            preferred_element_type=F32,
        ).reshape(4, 128, 128)
        stem = (fine_v[pl.ds(i * 4, 4)].astype(F32) + lifted).astype(BF)
        stem_v[pl.ds(i * 4, 4)] = stem
        for k in range(4):
            row = i * 4 + k + 2
            pad_stem[pl.ds(pl.multiple_of(row * PITCH, 16) + 8, 128), :] = stem[k].astype(F32)
            shifted_row(pad_stem, x3_stem, row)
        return carry

    lax.fori_loop(0, 8, stem_step, 0)
    fill_edges(pad_stem, 1)
    stem_halos = halo_copies(1, stem_v.at[0:2], stem_v.at[30:32])
    for copy in stem_halos:
        copy.start()

    has_up = (r > 0).astype(F32)
    has_down = (r < n_row - 1).astype(F32)
    has_left = (c > 0).astype(F32)
    has_right = (c < n_col - 1).astype(F32)

    def take_halos(which, pad, x3):
        for side, (row, there) in enumerate(((0, has_up), (34, has_down))):
            for k in range(2):
                pad[pl.ds((row + k) * PITCH + 8, 128), :] = (
                    land_row[which, side, k].astype(F32) * there
                )
        for side, (column, there) in enumerate(((6, has_left), (136, has_right))):
            for j in range(2):
                pad[pl.ds(2 * PITCH + column + j, 32, stride=PITCH), :] = (
                    land_col[which, side, j].astype(F32) * there
                )
        for corner in range(4):
            low, side = divmod(corner, 2)
            there = (has_up, has_down)[low] * (has_left, has_right)[side]
            for j in range(2):
                tile = land_corner[which, corner, j].astype(F32) * there
                for k in range(2):
                    source = k if low else 14 + k
                    row = 34 + k if low else k
                    column = (6, 136)[side] + j
                    pad[pl.ds(row * PITCH + column, 1), :] = tile[source : source + 1]
        for row in (0, 1, 34, 35):
            shifted_row(pad, x3, row)

        def patch(row, carry):
            base = pl.multiple_of(row * 128, 128)
            start = row * PITCH + 8
            x3[pl.ds(base, 16), 0:128] = pad[pl.ds(start - 1, 16), :].astype(BF)
            x3[pl.ds(base + 112, 16), 256:384] = pad[pl.ds(start + 113, 16), :].astype(BF)
            return carry

        lax.fori_loop(2, 34, patch, 0)

    for copy in cot_halos:
        copy.wait()
    take_halos(0, pad_cot, x3_cot)
    side_grad = side_conv(pad_cot, wp_second_f)
    parts = ((0, 9), (9, 8))
    for begin, pairs in parts:
        pair = pair_conv(x3_cot, wp_second_f, 2 * begin, pairs)
        for p in range(pairs):
            for k in range(2):
                grad_act[rows_of(2 * (begin + p) + k), :] = pair[
                    p * 128 : (p + 1) * 128, k * 128 : (k + 1) * 128
                ]

    for copy in stem_halos:
        copy.wait()
    take_halos(1, pad_stem, x3_stem)

    side_act, side_pre = gate(side_conv(pad_stem, wp_first), side_grad)
    for side, (column, there) in enumerate(((7, has_left), (136, has_right))):
        where = pl.ds(PITCH + column, 40, stride=PITCH)
        pad_act[where, :] = side_act[side * 40 : side * 40 + 40] * there
        pad_pre[where, :] = side_pre[side * 40 : side * 40 + 40] * there
    for begin, pairs in parts:
        pair = pair_conv(x3_stem, wp_first, 2 * begin, pairs)
        for p in range(pairs):
            for k in range(2):
                row = 2 * (begin + p) + k
                act, pre = gate(
                    pair[p * 128 : (p + 1) * 128, k * 128 : (k + 1) * 128],
                    grad_act[rows_of(row), :],
                )
                where = pl.ds((row + 1) * PITCH + 8, 128)
                pad_act[where, :] = act
                pad_pre[where, :] = pre
                pre_z[row + 1] = pre.astype(BF)

    blank = jnp.zeros((PITCH, 128), F32)

    @pl.when(r == 0)
    def _():
        pad_act[pl.ds(PITCH, PITCH), :] = blank
        pad_pre[pl.ds(PITCH, PITCH), :] = blank

    @pl.when(r == n_row - 1)
    def _():
        pad_act[pl.ds(34 * PITCH, PITCH), :] = blank
        pad_pre[pl.ds(34 * PITCH, PITCH), :] = blank

    pre_z[1] = jnp.zeros((128, 128), BF)
    pre_z[34] = jnp.zeros((128, 128), BF)

    def shift_step(row, carry):
        shifted_row(pad_act, x3_act, row)
        shifted_row(pad_pre, x3_pre, row)
        return carry

    lax.fori_loop(1, 35, shift_step, 0)

    def tap_grad(x3, grad, group):
        total = None
        for begin, rows in ((1, 12), (13, 12), (25, 10)):
            lhs = x3[rows_of(begin, rows), :]
            rhs = jnp.concatenate(
                [
                    grad[pl.ds(begin + 1 - a, rows)].reshape(rows * 128, 128)
                    for a in range(3)
                ],
                1,
            )
            part = lax.dot_general(
                lhs, rhs, (((0,), (0,)), ((), ())), preferred_element_type=F32
            )
            if begin == 1:
                taps[...] = part
            else:
                taps[...] += part
        for a in range(3):
            local[group, a * 384 : (a + 1) * 384] = taps[:, a * 128 : (a + 1) * 128].astype(BF)

    half_rows = nq * CHUNK

    def step0(group):
        return pltpu.make_async_remote_copy(
            local.at[group, pl.ds(pl.multiple_of((1 - h) * half_rows, 16), half_rows)],
            land0.at[group],
            s0_send.at[group],
            s0_recv.at[group],
            (r, sibling),
            MESH,
        )

    def step1(group):
        return [
            pltpu.make_async_remote_copy(
                half.at[group, peer],
                land1.at[group, q],
                s1_send.at[group, peer],
                s1_recv.at[group, q],
                (r, 2 * peer + h),
                MESH,
            )
            for peer in q_peers
        ]

    def step2(group):
        return [
            pltpu.make_async_remote_copy(
                land2.at[group, r],
                land2.at[group, r],
                s2_send.at[group, peer],
                s2_recv.at[group, r],
                (peer, c),
                MESH,
            )
            for peer in r_peers
        ]

    def step3(group):
        return [
            pltpu.make_async_remote_copy(
                final.at[group, own],
                final.at[group, own],
                s3_send.at[group, peer],
                s3_recv.at[group, q],
                (r, 2 * peer + h),
                MESH,
            )
            for peer in q_peers
        ]

    def step4(group):
        mine = final.at[group, pl.ds(h * nq, nq)]
        return pltpu.make_async_remote_copy(
            mine, mine, s4_send.at[group], s4_recv.at[group], (r, sibling), MESH
        )

    def await_slots(land, sem, slots, where):
        for slot in slots:
            pltpu.make_async_remote_copy(
                land.at[where(slot)], land.at[where(slot)], sem.at[slot], sem.at[slot],
                (r, sibling), MESH,
            ).wait_recv()

    def start_all(copies):
        for copy in copies:
            copy.start()

    def end_step0(group, copy):
        copy.wait()
        for k in range(nq):
            mine = local[
                group, pl.ds(pl.multiple_of(h * half_rows + k * CHUNK, 16), CHUNK)
            ].astype(F32)
            theirs = land0[group, k * CHUNK : (k + 1) * CHUNK].astype(F32)
            half[group, k] = (mine + theirs).astype(BF)
        sends = step1(group)
        start_all(sends)
        return sends

    def end_step1(group, sends):
        await_slots(land1.at[group], s1_recv.at[group], q_peers, lambda s: s)
        land1[group, q] = half[group, q]
        total = land1[group, 0].astype(F32)
        for k in range(1, nq):
            total = total + land1[group, k].astype(F32)
        land2[group, r] = total.astype(BF)
        for copy in sends:
            copy.wait_send()
        sends = step2(group)
        start_all(sends)
        return sends

    def end_step2(group, sends):
        await_slots(land2.at[group], s2_recv.at[group], r_peers, lambda s: s)
        if group < 2:
            total = land2[group, 0].astype(F32)
            for k in range(1, n_row):
                total = total + land2[group, k].astype(F32)
            final[group, own] = (total * (1.0 / 1024.0)).astype(BF)
        else:
            total = land2[group, 0, 48:80].astype(F32)
            for k in range(1, n_row):
                total = total + land2[group, k, 48:80].astype(F32)
            lift_wide[...] = total * (1.0 / 1024.0)
            owned = (
                land2[group, r, 16:32].astype(F32)
                + land2[group, up, 32:48].astype(F32) * has_up
                + land2[group, down, 0:16].astype(F32) * has_down
            )
            final[group, own, 0:16] = owned.astype(BF)
            final[group, own, 16:80] = jnp.zeros((64, 128), BF)
        for copy in sends:
            copy.wait_send()
        sends = step3(group)
        start_all(sends)
        return sends

    def end_step3(group, sends):
        await_slots(final.at[group], s3_recv.at[group], q_peers, lambda s: h * nq + s)
        for copy in sends:
            copy.wait_send()
        copy = step4(group)
        copy.start()
        return copy

    def end_step4(group, copy):
        copy.wait_send()
        theirs = final.at[group, pl.ds((1 - h) * nq, nq)]
        pltpu.make_async_remote_copy(
            theirs, theirs, s4_send.at[group], s4_recv.at[group], (r, sibling), MESH
        ).wait_recv()

    tap_grad(x3_act, cot_z, 0)
    pend_a = step0(0)
    pend_a.start()
    tap_grad(x3_stem, pre_z, 1)
    pend_a = end_step0(0, pend_a)
    pend_b = step0(1)
    pend_b.start()

    for part in range(2):
        pair = pair_conv(x3_pre, wp_first_f, 1 + 16 * part, 8)
        for p in range(8):
            for k in range(2):
                row = 16 * part + 2 * p + k
                gf_v[row] = (
                    pair[p * 128 : (p + 1) * 128, k * 128 : (k + 1) * 128] + cot_rows(row + 2)
                ).astype(BF)
    gf_copy = pltpu.make_async_copy(gf_v, grad_fine, out_sem.at[0])
    gf_copy.start()
    pend_a = end_step1(0, pend_a)
    pend_b = end_step0(1, pend_b)

    moment = jnp.zeros((512, 128), F32)
    for part in range(4):
        moment = moment + jnp.dot(
            weights_it[:, part * 1024 : (part + 1) * 1024],
            gf_v[part * 8 : part * 8 + 8].reshape(1024, 128),
            preferred_element_type=F32,
        )
    high = moment.astype(BF)
    rest = (moment - high.astype(F32)).astype(BF)
    lift_part = jnp.dot(picked, high, preferred_element_type=F32) + jnp.dot(
        picked, rest, preferred_element_type=F32
    )
    across = (((1,), (1,)), ((), ()))
    blocks = lax.dot_general(
        lift_v[...], high, across, preferred_element_type=F32
    ) + lax.dot_general(lift_v[...], rest, across, preferred_element_type=F32)
    lift_part = lift_part.astype(BF)
    for section in range(3):
        for n in range(8):
            value = jnp.zeros((32, 128), F32)
            for k in range(4):
                value = value + jnp.where(
                    local_ids[k] == section * 8 + n, blocks[:, k * 128 : (k + 1) * 128], 0.0
                )
            value = value.astype(BF)
            for side in range(2):
                low = (2 * n + side) * CHUNK + section * 16
                local[2, low : low + 16] = value[side * 16 : side * 16 + 16]
    for owner in range(n_col):
        local[2, owner * CHUNK + 48 : owner * CHUNK + 80] = lift_part
    pend_c = step0(2)
    pend_c.start()
    pend_a = end_step2(0, pend_a)
    pend_b = end_step1(1, pend_b)

    for part in range(2):
        pair = pair_conv(x3_act, wp_second, 1 + 16 * part, 8)
        for p in range(8):
            for k in range(2):
                row = 16 * part + 2 * p + k
                out_v[row] = (
                    pair[p * 128 : (p + 1) * 128, k * 128 : (k + 1) * 128]
                    + stem_v[row].astype(F32)
                ).astype(BF)
        if part == 0:
            pend_c = end_step0(2, pend_c)
    out_copy = pltpu.make_async_copy(out_v, out, out_sem.at[1])
    out_copy.start()

    pend_a = end_step3(0, pend_a)
    pend_b = end_step2(1, pend_b)
    pend_c = end_step1(2, pend_c)
    end_step4(0, pend_a)

    def widen(group, target, sem):
        for a in range(3):
            for e in range(3):
                for part in range(8):
                    low = (a * 3 + e) * 128 + part * 16
                    owner, at = divmod(low, CHUNK)
                    wide[group, a, e, part * 16 : part * 16 + 16] = final[
                        group, owner, at : at + 16
                    ].astype(F32)
        copy = pltpu.make_async_copy(wide.at[group], target, sem)
        copy.start()
        return copy

    wide_a = widen(0, grad_second, out_sem.at[2])
    pend_b = end_step3(1, pend_b)
    pend_c = end_step2(2, pend_c)
    lift_copy = pltpu.make_async_copy(lift_wide, grad_lift, out_sem.at[3])
    lift_copy.start()
    end_step4(1, pend_b)
    wide_b = widen(1, grad_first, out_sem.at[4])
    pend_c = end_step3(2, pend_c)
    end_step4(2, pend_c)
    for n in range(8):
        for side in range(2):
            coarse_wide[n, side * 16 : side * 16 + 16] = final[2, 2 * n + side, 0:16].astype(F32)
    coarse_copy = pltpu.make_async_copy(coarse_wide, grad_coarse, out_sem.at[5])
    coarse_copy.start()
    for copy in (gf_copy, out_copy, wide_a, lift_copy, wide_b, coarse_copy):
        copy.wait()


def body(n_row, n_col, fine, coarse, block_map, interp, lift, first, second, cot):
    anywhere = pl.BlockSpec(memory_space=pl.ANY)
    nq = n_col // 2
    dma = pltpu.SemaphoreType.DMA

    def vm(shape, dtype=BF):
        return pltpu.VMEM(shape, dtype)

    pad = vm((42 * PITCH, 128), F32)
    x3 = vm((36 * 128, 384))
    wp = vm((1536, 256))
    tile = vm((32, 128, 128))
    scratch = [
        tile,
        vm((4, 128, 32, 128)),
        vm((512, 4096)),
        vm((24, 32, 128)),
        vm((32, 128)),
        vm((3, 3, 128, 128)),
        vm((3, 3, 128, 128)),
        wp, wp, wp, wp,
        pad, pad, pad, pad,
        x3, x3, x3, x3,
        vm((36, 128, 128)),
        vm((36, 128, 128)),
        tile,
        vm((34 * 128, 128), F32),
        tile,
        tile,
        vm((512, 128)),
        vm((2, 2, 2, 32, 128)),
        vm((2, 2, 2, 128, 128)),
        vm((2, 2, 2, 32, 128)),
        vm((2, 4, 2, 16, 128)),
        vm((384, 384), F32),
        vm((3, n_col * CHUNK, 128)),
        vm((3, nq * CHUNK, 128)),
        vm((3, nq, CHUNK, 128)),
        vm((3, nq, CHUNK, 128)),
        vm((3, n_row, CHUNK, 128)),
        vm((3, n_col, CHUNK, 128)),
        vm((2, 3, 3, 128, 128), F32),
        vm((8, 32, 128), F32),
        vm((32, 128), F32),
        dma((7,)), dma((6,)),
        dma((2,)), dma((2,)),
        dma((2, 8)), dma((2, 8)),
        dma((3,)), dma((3,)),
        dma((3, nq)), dma((3, nq)),
        dma((3, n_row)), dma((3, n_row)),
        dma((3, nq)), dma((3, nq)),
        dma((3,)), dma((3,)),
    ]
    shapes = (
        jax.ShapeDtypeStruct(fine.shape, BF),
        jax.ShapeDtypeStruct(fine.shape, BF),
        jax.ShapeDtypeStruct(coarse.shape, F32),
        jax.ShapeDtypeStruct(first.shape, F32),
        jax.ShapeDtypeStruct(second.shape, F32),
        jax.ShapeDtypeStruct(lift.shape, F32),
    )
    return pl.pallas_call(
        functools.partial(kernel, n_row, n_col),
        out_shape=shapes,
        in_specs=[
            anywhere, anywhere, pl.BlockSpec(memory_space=pltpu.SMEM),
            anywhere, anywhere, anywhere, anywhere, anywhere,
        ],
        out_specs=tuple([anywhere] * 6),
        scratch_shapes=scratch,
        compiler_params=pltpu.CompilerParams(
            collective_id=0, has_side_effects=True, vmem_limit_bytes=62 * 1024 * 1024
        ),
        name="step",
    )(fine, coarse, block_map.reshape(-1), interp, lift, first, second, cot)


def solution(mesh):
    n_row, n_col = mesh.shape["row"], mesh.shape["col"]
    return jax.shard_map(
        functools.partial(body, n_row, n_col),
        mesh=mesh,
        in_specs=(
            P("row", "col", None),
            P("row", None, None),
            P("row", "col", None),
            P(None, None, "row", "col"),
            P(),
            P(),
            P(),
            P("row", "col", None),
        ),
        out_specs=(
            P("row", "col", None),
            P("row", "col", None),
            P("row", None, None),
            P(),
            P(),
            P(),
        ),
        check_vma=False,
    )
```

time: 486 us -> 73.1 us (0.15); the launches traced: 478 us -> 72.9 us
  waiting for transfers between devices: 195 us -> 0 us
  blocking collectives: 70.8 us -> 0 us
  starting transfers between devices: 66.5 us -> 0 us
  Pallas kernels: 0 us -> 64.6 us
  matrix products: 46.5 us -> 0 us
  local copies, waits for them, and re-layouts: 50.8 us -> 7.62 us
  other arithmetic: 24.9 us -> 0 us
  between operations: 23.2 us -> 0.68 us
    psum x2 -> x0, waiting for transfers between devices: 187 us -> none  [the longest x1 113 us: body(): grad_coarse = lax.psum(owned, 'col')]
    psum x1 -> x0, blocking collectives: 70.8 us -> none  [body(): lax.psum((first_local, second_local, lift_local), ('row', 'col'))]
    ppermute x20 -> x0, starting transfers between devices: 66.4 us -> none  [the longest x9 42.3 us: extended(): lax.ppermute(tail, axis, [(i, (i + 1) % count) for i in range(ends)])]
    pallas_call x0 -> x1, Pallas kernels: none -> 64.6 us  [body(): pl.pallas_call(functools.partial(kernel, n_row, n_col), out_shape=shapes,...]
    dot_general x65 -> x0, matrix products: 46.5 us -> none  [the longest x36 32.9 us: conv_taps(): jnp.dot(piece, kernel[shift_row, shift_col], preferred_element_type=jnp.f...]
    slice x24 -> x0, local copies, waits for them, and re-layouts: 35.3 us -> none  [the longest x13 20.3 us: conv_taps(): padded[shift_row:shift_row + rows, shift_col:shift_col + cols]]
    concatenate x8 -> x0, other arithmetic: 11.9 us -> none  [extended(): jnp.concatenate([lax.ppermute(tail, axis, [(i, (i + 1) % count) for i in...]
    ppermute x20 -> x0, waiting for transfers between devices: 8.18 us -> none  [the longest x9 8.15 us: extended(): lax.ppermute(head, axis, [((i + 1) % count, i) for i in range(ends)])]
  transfers between devices with their start and end apart: 22 -> 0, of which waited for: 5 -> 0; matrix products, arithmetic and copies ran while one was open for 19% -> 0% of each run, Pallas kernels for 0% -> 0%
where the time goes in v1:
time: 73.1 us; the launch traced here: 72.9 us
  Pallas kernels  64.6 us (88%)
  local copies, waits for them, and re-layouts  7.62 us (10%)
    pallas_call x1, Pallas kernels, body(): pl.pallas_call(functools.partial(kernel, n_row, n_col), out_shape=shapes,...  64.6 us
    unnamed x14, local copies, waits for them, and re-layouts  7.62 us

profile of v1, /device:TPU:1, one launch (start us, length us, event | category | flops | bytes accessed | tf_op | source)
XLA Modules:
  0.0 72.9 jit_solution(11522433962142488144)
XLA Ops:
  0.6 64.6 %step.1 = (bf16[32,128,128]{2,1,0:T(8,128)(2,1)}, bf16[32,128,128]{2,1,0:T(8,128)(2,1)}, f32[8,32,128]{2,1,0:T(8,128)}, f32[3,3,128,128]{3,2,1,0:T(8,128)}, f32[...) custom-call(bf16[32,128,128]{2,1,0:T(8,128)(2,1)} %fine.1, bf16[8,32,128]{2,1,0:T(8,128)(2,1)} %coarse.1, s32[4]{0:T(128)} %bitcast.1, ...), custom_call_target="tpu_custom_call" | custom-call | tf_op jit(solution)/shard_map/step/pallas_call | solution.py:711
  65.2 0.0 copy-start.2
  65.2 0.0 copy-start.1
  65.3 0.0 copy-start
  65.3 0.0 copy-start.3
  65.3 2.4 %copy.20 = bf16[32,128,128]{2,1,0:T(8,128)(2,1)} copy(bf16[32,128,128]{2,1,0:T(8,128)(2,1)} %get-tuple-element.12) | data formatting | bytes 2097152
  67.7 2.3 %copy.21 = bf16[32,128,128]{2,1,0:T(8,128)(2,1)} copy(bf16[32,128,128]{2,1,0:T(8,128)(2,1)} %get-tuple-element.13) | data formatting | bytes 2097152
  70.0 0.0 copy-done.2
  70.0 0.7 copy.22
  70.6 0.0 copy-done.1
  70.7 0.8 %copy.23 = f32[3,3,128,128]{3,2,1,0:T(8,128)} copy(f32[3,3,128,128]{3,2,1,0:T(8,128)S(1)} %copy-done.1) | data formatting | bytes 1179648
  71.5 0.0 copy-done
  71.5 0.8 %copy.24 = f32[3,3,128,128]{3,2,1,0:T(8,128)} copy(f32[3,3,128,128]{3,2,1,0:T(8,128)S(1)} %copy-done) | data formatting | bytes 1179648
  72.3 0.0 copy-done.3
  72.3 0.6 copy.25
Async XLA Ops:
  65.2 4.8 %copy-start.2 = (f32[8,32,128]{2,1,0:T(8,128)S(1)}, f32[8,32,128]{2,1,0:T(8,128)}, u32[]{:S(2)}) copy-start(f32[8,32,128]{2,1,0:T(8,128)} %get-tuple-element.14) | copy-start | bytes 393220
  65.2 5.4 %copy-start.1 = (f32[3,3,128,128]{3,2,1,0:T(8,128)S(1)}, f32[3,3,128,128]{3,2,1,0:T(8,128)}, u32[]{:S(2)}) copy-start(f32[3,3,128,128]{3,2,1,0:T(8,128)} %get-tuple-element.15) | copy-start | bytes 1769476
  65.3 6.2 %copy-start = (f32[3,3,128,128]{3,2,1,0:T(8,128)S(1)}, f32[3,3,128,128]{3,2,1,0:T(8,128)}, u32[]{:S(2)}) copy-start(f32[3,3,128,128]{3,2,1,0:T(8,128)} %get-tuple-element.16) | copy-start | bytes 1769476
  65.3 7.0 %copy-start.3 = (f32[32,128]{1,0:T(8,128)S(1)}, f32[32,128]{1,0:T(8,128)}, u32[]{:S(2)}) copy-start(f32[32,128]{1,0:T(8,128)} %get-tuple-element.17) | copy-start | bytes 49156

commit v2 on v1

--- a/solution.py
+++ b/solution.py
@@ -99,8 +99,6 @@
     pre_z,
     stem_v,
     grad_act,
-    gf_v,
-    out_v,
     mix,
     edge_send,
     land_row,
@@ -113,11 +111,7 @@
     land1,
     land2,
     final,
-    wide,
-    coarse_wide,
-    lift_wide,
     copy_sem,
-    out_sem,
     coarse_send,
     coarse_recv,
     halo_send,
@@ -512,7 +506,7 @@
             total = land2[group, 0, 48:80].astype(F32)
             for k in range(1, n_row):
                 total = total + land2[group, k, 48:80].astype(F32)
-            lift_wide[...] = total * (1.0 / 1024.0)
+            grad_lift[...] = total * (1.0 / 1024.0)
             owned = (
                 land2[group, r, 16:32].astype(F32)
                 + land2[group, up, 32:48].astype(F32) * has_up
@@ -554,11 +548,9 @@
         for p in range(8):
             for k in range(2):
                 row = 16 * part + 2 * p + k
-                gf_v[row] = (
+                grad_fine[row] = (
                     pair[p * 128 : (p + 1) * 128, k * 128 : (k + 1) * 128] + cot_rows(row + 2)
                 ).astype(BF)
-    gf_copy = pltpu.make_async_copy(gf_v, grad_fine, out_sem.at[0])
-    gf_copy.start()
     pend_a = end_step1(0, pend_a)
     pend_b = end_step0(1, pend_b)
 
@@ -566,7 +558,7 @@
     for part in range(4):
         moment = moment + jnp.dot(
             weights_it[:, part * 1024 : (part + 1) * 1024],
-            gf_v[part * 8 : part * 8 + 8].reshape(1024, 128),
+            grad_fine[part * 8 : part * 8 + 8].reshape(1024, 128),
             preferred_element_type=F32,
         )
     high = moment.astype(BF)
@@ -602,48 +594,53 @@
         for p in range(8):
             for k in range(2):
                 row = 16 * part + 2 * p + k
-                out_v[row] = (
+                out[row] = (
                     pair[p * 128 : (p + 1) * 128, k * 128 : (k + 1) * 128]
                     + stem_v[row].astype(F32)
                 ).astype(BF)
         if part == 0:
             pend_c = end_step0(2, pend_c)
-    out_copy = pltpu.make_async_copy(out_v, out, out_sem.at[1])
-    out_copy.start()
 
     pend_a = end_step3(0, pend_a)
     pend_b = end_step2(1, pend_b)
     pend_c = end_step1(2, pend_c)
     end_step4(0, pend_a)
 
-    def widen(group, target, sem):
+    def widen(group, target):
         for a in range(3):
             for e in range(3):
                 for part in range(8):
                     low = (a * 3 + e) * 128 + part * 16
                     owner, at = divmod(low, CHUNK)
-                    wide[group, a, e, part * 16 : part * 16 + 16] = final[
+                    target[a, e, part * 16 : part * 16 + 16] = final[
                         group, owner, at : at + 16
                     ].astype(F32)
-        copy = pltpu.make_async_copy(wide.at[group], target, sem)
-        copy.start()
-        return copy
-
-    wide_a = widen(0, grad_second, out_sem.at[2])
+
+    widen(0, grad_second)
     pend_b = end_step3(1, pend_b)
     pend_c = end_step2(2, pend_c)
-    lift_copy = pltpu.make_async_copy(lift_wide, grad_lift, out_sem.at[3])
-    lift_copy.start()
     end_step4(1, pend_b)
-    wide_b = widen(1, grad_first, out_sem.at[4])
+    widen(1, grad_first)
     pend_c = end_step3(2, pend_c)
     end_step4(2, pend_c)
     for n in range(8):
         for side in range(2):
-            coarse_wide[n, side * 16 : side * 16 + 16] = final[2, 2 * n + side, 0:16].astype(F32)
-    coarse_copy = pltpu.make_async_copy(coarse_wide, grad_coarse, out_sem.at[5])
-    coarse_copy.start()
-    for copy in (gf_copy, out_copy, wide_a, lift_copy, wide_b, coarse_copy):
+            grad_coarse[n, side * 16 : side * 16 + 16] = final[2, 2 * n + side, 0:16].astype(F32)
+
+
+def hand_over(*refs):
+    sems = refs[12]
+    copies = []
+    for k in range(6):
+        source, target = refs[k], refs[6 + k]
+        pieces = 4 if k < 2 else 1
+        size = source.shape[0] // pieces
+        for p in range(pieces):
+            part = pl.ds(p * size, size)
+            copies.append(pltpu.make_async_copy(source.at[part], target.at[part], sems.at[k, p]))
+    for copy in copies:
+        copy.start()
+    for copy in copies:
         copy.wait()
 
 
@@ -674,8 +671,6 @@
         vm((36, 128, 128)),
         tile,
         vm((34 * 128, 128), F32),
-        tile,
-        tile,
         vm((512, 128)),
         vm((2, 2, 2, 32, 128)),
         vm((2, 2, 2, 128, 128)),
@@ -688,10 +683,7 @@
         vm((3, nq, CHUNK, 128)),
         vm((3, n_row, CHUNK, 128)),
         vm((3, n_col, CHUNK, 128)),
-        vm((2, 3, 3, 128, 128), F32),
-        vm((8, 32, 128), F32),
-        vm((32, 128), F32),
-        dma((7,)), dma((6,)),
+        dma((7,)),
         dma((2,)), dma((2,)),
         dma((2, 8)), dma((2, 8)),
         dma((3,)), dma((3,)),
@@ -700,28 +692,40 @@
         dma((3, nq)), dma((3, nq)),
         dma((3,)), dma((3,)),
     ]
+    def handed(shape, dtype):
+        return pltpu.VMEM(shape, dtype)
+
     shapes = (
-        jax.ShapeDtypeStruct(fine.shape, BF),
-        jax.ShapeDtypeStruct(fine.shape, BF),
-        jax.ShapeDtypeStruct(coarse.shape, F32),
-        jax.ShapeDtypeStruct(first.shape, F32),
-        jax.ShapeDtypeStruct(second.shape, F32),
-        jax.ShapeDtypeStruct(lift.shape, F32),
+        handed(fine.shape, BF),
+        handed(fine.shape, BF),
+        handed(coarse.shape, F32),
+        handed(first.shape, F32),
+        handed(second.shape, F32),
+        handed(lift.shape, F32),
     )
-    return pl.pallas_call(
+    results = pl.pallas_call(
         functools.partial(kernel, n_row, n_col),
         out_shape=shapes,
         in_specs=[
             anywhere, anywhere, pl.BlockSpec(memory_space=pltpu.SMEM),
             anywhere, anywhere, anywhere, anywhere, anywhere,
         ],
-        out_specs=tuple([anywhere] * 6),
+        out_specs=tuple([pl.BlockSpec(memory_space=pltpu.VMEM)] * 6),
         scratch_shapes=scratch,
         compiler_params=pltpu.CompilerParams(
-            collective_id=0, has_side_effects=True, vmem_limit_bytes=62 * 1024 * 1024
+            collective_id=0, has_side_effects=True, vmem_limit_bytes=56 * 1024 * 1024
         ),
         name="step",
     )(fine, coarse, block_map.reshape(-1), interp, lift, first, second, cot)
+    return pl.pallas_call(
+        hand_over,
+        out_shape=tuple(jax.ShapeDtypeStruct(x.shape, x.dtype) for x in results),
+        in_specs=[pl.BlockSpec(memory_space=pltpu.VMEM)] * 6,
+        out_specs=tuple([anywhere] * 6),
+        scratch_shapes=[dma((6, 4))],
+        name="hand_over",
+        compiler_params=pltpu.CompilerParams(vmem_limit_bytes=1024 * 1024),
+    )(*results)
 
 
 def solution(mesh):

time: 73.1 us -> 66.8 us (0.914)
  local copies, waits for them, and re-layouts: 7.62 us -> 0 us
  Pallas kernels: 64.6 us -> 65.9 us
    unnamed x14 -> x0, local copies, waits for them, and re-layouts: 7.62 us -> none
    pallas_call x0 -> x1, Pallas kernels: none -> 1.96 us  [body(): pl.pallas_call(hand_over, out_shape=tuple((jax.ShapeDtypeStruct(x.shape,...]
where the time goes in v2:
time: 66.8 us; the launch traced here: 66.7 us
  Pallas kernels  65.9 us (99%)
  between operations  0.8 us (1%)
    pallas_call x1, Pallas kernels, body(): pl.pallas_call(functools.partial(kernel, n_row, n_col), out_shape=shapes,...  63.9 us
    pallas_call x1, Pallas kernels, body(): pl.pallas_call(hand_over, out_shape=tuple((jax.ShapeDtypeStruct(x.shape,...  1.96 us

profile of v2, /device:TPU:1, one launch (start us, length us, event | category | flops | bytes accessed | tf_op | source)
XLA Modules:
  0.0 66.7 jit_solution(466328758766945235)
XLA Ops:
  0.6 63.9 %step.1 = (bf16[32,128,128]{2,1,0:T(8,128)(2,1)S(1)}, bf16[32,128,128]{2,1,0:T(8,128)(2,1)S(1)}, f32[8,32,128]{2,1,0:T(8,128)S(1)}, f32[3,3,128,128]{3,2,1,0:T(8...) custom-call(bf16[32,128,128]{2,1,0:T(8,128)(2,1)} %fine.1, bf16[8,32,128]{2,1,0:T(8,128)(2,1)} %coarse.1, ...), custom_call_target="tpu_custom_call" | custom-call | tf_op jit(solution)/shard_map/step/pallas_call | solution.py:706
  64.6 2.0 %hand_over.1 = (bf16[32,128,128]{2,1,0:T(8,128)(2,1)}, bf16[32,128,128]{2,1,0:T(8,128)(2,1)}, f32[8,32,128]{2,1,0:T(8,128)}, f32[3,3,128,128]{3,2,1,0:T(8,128)},...) custom-call(bf16[32,128,128]{2,1,0:T(8,128)(2,1)S(1)} %get-tuple-element.12.refs_0_, ...), custom_call_target="tpu_custom_call" | custom-call | tf_op jit(solution)/shard_map/hand_over/pallas_call | solution.py:720

commit v3 on v2

--- a/solution.py
+++ b/solution.py
@@ -21,22 +21,23 @@
     return pl.ds(start, count * pitch)
 
 
-def pair_conv(x3, wp, first, pairs):
+def pair_conv(x3, wp, starts):
     parts = []
     for j in range(4):
-        parts.append(
-            jnp.concatenate([x3[rows_of(first + 2 * p + j), :] for p in range(pairs)], 0)
-        )
+        parts.append(jnp.concatenate([x3[rows_of(start + j), :] for start in starts], 0))
     return jnp.dot(jnp.concatenate(parts, 1), wp[...], preferred_element_type=F32)
+
+
+SIDES = (7, 8, 135, 136)
 
 
 def side_conv(pad, wp):
     sides = []
-    for base in (6, 135):
+    for column in SIDES:
         sides.append(
             jnp.concatenate(
                 [
-                    pad[pl.ds(a * PITCH + base + e, 40, stride=PITCH), :].astype(BF)
+                    pad[pl.ds(a * PITCH + column - 1 + e, 40, stride=PITCH), :].astype(BF)
                     for a in range(3)
                     for e in range(3)
                 ],
@@ -160,39 +161,43 @@
         pltpu.make_async_copy(first, first_v, copy_sem.at[2]),
         pltpu.make_async_copy(second, second_v, copy_sem.at[3]),
         pltpu.make_async_copy(lift, lift_v, copy_sem.at[4]),
-        pltpu.make_async_copy(interp, interp_v, copy_sem.at[5]),
-        pltpu.make_async_copy(fine, fine_v, copy_sem.at[6]),
+        pltpu.make_async_copy(fine, fine_v, copy_sem.at[5]),
     ]
-    for copy in copies:
+    slot_copies = [
+        pltpu.make_async_copy(interp.at[k], interp_v.at[k], copy_sem.at[6 + k]) for k in range(4)
+    ]
+    for copy in copies[0:5] + slot_copies + copies[5:6]:
         copy.start()
-
-    def cot_rows(row):
-        return cot_z[row].astype(F32)
 
     zero_row = jnp.zeros((2, 128, 128), BF)
     cot_z[0:2] = zero_row
     cot_z[34:36] = zero_row
     pre_z[0:2] = zero_row
     pre_z[34:36] = zero_row
-    copies[0].wait()
-
-    def cot_step(i, carry):
-        pad_cot[pl.ds(pl.multiple_of(i * PITCH, 16) + 8, 128), :] = cot_rows(i)
-        shifted_row(pad_cot, x3_cot, i)
-        return carry
-
-    lax.fori_loop(2, 34, cot_step, 0)
-
-    def fill_edges(pad, which):
-        for side, columns in enumerate(((0, 1), (126, 127))):
-            for j, x in enumerate(columns):
-                edge_send[which, side, j] = pad[
-                    pl.ds(2 * PITCH + 8 + x, 32, stride=PITCH), :
-                ].astype(BF)
-
-    fill_edges(pad_cot, 0)
+
+    def halo_copy(which, k, src, dst, device):
+        return pltpu.make_async_remote_copy(
+            src, dst, halo_send.at[which, k], halo_recv.at[which, k], device, MESH
+        )
+
+    def row_halos(which, source):
+        return [
+            halo_copy(which, 0, source.at[0:2], land_row.at[which, 1], (up, c)),
+            halo_copy(which, 1, source.at[30:32], land_row.at[which, 0], (down, c)),
+        ]
+
+    def column_halos(which):
+        edges = edge_send.at[which]
+        return [
+            halo_copy(which, 2, edges.at[0], land_col.at[which, 1], (r, left)),
+            halo_copy(which, 3, edges.at[1], land_col.at[which, 0], (r, right)),
+            halo_copy(which, 4, edges.at[0, :, 0:16], land_corner.at[which, 3], (up, left)),
+            halo_copy(which, 5, edges.at[1, :, 0:16], land_corner.at[which, 2], (up, right)),
+            halo_copy(which, 6, edges.at[0, :, 16:32], land_corner.at[which, 1], (down, left)),
+            halo_copy(which, 7, edges.at[1, :, 16:32], land_corner.at[which, 0], (down, right)),
+        ]
+
     pl.semaphore_wait(barrier, len(peers))
-
     coarse_copies = [
         pltpu.make_async_remote_copy(
             coarse, window.at[16:24], coarse_send.at[0], coarse_recv.at[0], (up, c), MESH
@@ -201,30 +206,34 @@
             coarse, window.at[0:8], coarse_send.at[1], coarse_recv.at[1], (down, c), MESH
         ),
     ]
-    for copy in coarse_copies:
+    cot_halos = row_halos(0, cot)
+    for copy in coarse_copies + cot_halos:
         copy.start()
 
-    def halo_copies(which, head, tail):
-        def copy(k, src, dst, device):
-            return pltpu.make_async_remote_copy(
-                src, dst, halo_send.at[which, k], halo_recv.at[which, k], device, MESH
-            )
-
-        edges = edge_send.at[which]
-        return [
-            copy(0, head, land_row.at[which, 1], (up, c)),
-            copy(1, tail, land_row.at[which, 0], (down, c)),
-            copy(2, edges.at[0], land_col.at[which, 1], (r, left)),
-            copy(3, edges.at[1], land_col.at[which, 0], (r, right)),
-            copy(4, edges.at[0, :, 0:16], land_corner.at[which, 3], (up, left)),
-            copy(5, edges.at[1, :, 0:16], land_corner.at[which, 2], (up, right)),
-            copy(6, edges.at[0, :, 16:32], land_corner.at[which, 1], (down, left)),
-            copy(7, edges.at[1, :, 16:32], land_corner.at[which, 0], (down, right)),
-        ]
-
-    cot_halos = halo_copies(0, cot_z.at[2:4], cot_z.at[32:34])
-    for copy in cot_halos:
+    def cot_rows(row):
+        return cot_z[row].astype(F32)
+
+    copies[0].wait()
+
+    def cot_step(i, carry):
+        pad_cot[pl.ds(pl.multiple_of(i * PITCH, 16) + 8, 128), :] = cot_rows(i)
+        shifted_row(pad_cot, x3_cot, i)
+        return carry
+
+    lax.fori_loop(2, 34, cot_step, 0)
+
+    def fill_edges(pad, which):
+        for side, columns in enumerate(((0, 1), (126, 127))):
+            for j, x in enumerate(columns):
+                edge_send[which, side, j] = pad[
+                    pl.ds(2 * PITCH + 8 + x, 32, stride=PITCH), :
+                ].astype(BF)
+
+    fill_edges(pad_cot, 0)
+    cot_sides = column_halos(0)
+    for copy in cot_sides:
         copy.start()
+    cot_halos = cot_halos + cot_sides
 
     copies[2].wait()
     copies[3].wait()
@@ -241,21 +250,32 @@
                     target[low : low + 128, 0:128] = value
                     target[low + 384 : low + 512, 128:256] = value
 
-    copies[5].wait()
-
-    def turn(i, carry):
-        slot = lax.div(i, 4)
-        block = lax.rem(i, 4)
-        piece = jnp.swapaxes(interp_v[slot, pl.ds(block * 32, 32)], 0, 1)
-        for y in range(32):
-            weights_it[pl.ds(pl.multiple_of(i * 32, 32), 32), y * 128 : (y + 1) * 128] = piece[y]
-        return carry
-
-    lax.fori_loop(0, 16, turn, 0)
+    inner = (tuple(range(2, 18, 2)), tuple(range(18, 32, 2)))
+
+    def rows_of_pairs(pair, starts):
+        for p, start in enumerate(starts):
+            for k in range(2):
+                yield start + k, pair[p * 128 : (p + 1) * 128, k * 128 : (k + 1) * 128]
+
+    for starts in inner:
+        for row, value in rows_of_pairs(pair_conv(x3_cot, wp_second_f, starts), starts):
+            grad_act[rows_of(row), :] = value
+
+    for slot in range(4):
+        slot_copies[slot].wait()
+
+        def turn(i, carry, slot=slot):
+            piece = jnp.swapaxes(interp_v[slot, pl.ds(i * 32, 32)], 0, 1)
+            where = pl.ds(pl.multiple_of(slot * 128 + i * 32, 32), 32)
+            for y in range(32):
+                weights_it[where, y * 128 : (y + 1) * 128] = piece[y]
+            return carry
+
+        lax.fori_loop(0, 4, turn, 0)
 
     copies[1].wait()
     copies[4].wait()
-    copies[6].wait()
+    copies[5].wait()
     for copy in coarse_copies:
         copy.wait()
     local_ids = [jnp.clip(ids[k] - (r - 1) * 8, 0, 23) for k in range(4)]
@@ -279,11 +299,26 @@
             shifted_row(pad_stem, x3_stem, row)
         return carry
 
-    lax.fori_loop(0, 8, stem_step, 0)
-    fill_edges(pad_stem, 1)
-    stem_halos = halo_copies(1, stem_v.at[0:2], stem_v.at[30:32])
+    stem_step(0, 0)
+    stem_step(7, 0)
+    stem_halos = row_halos(1, stem_v)
     for copy in stem_halos:
         copy.start()
+    lax.fori_loop(1, 7, stem_step, 0)
+    fill_edges(pad_stem, 1)
+    stem_sides = column_halos(1)
+    for copy in stem_sides:
+        copy.start()
+    stem_halos = stem_halos + stem_sides
+
+    def put(row, act, pre):
+        where = pl.ds((row + 1) * PITCH + 8, 128)
+        pad_act[where, :] = act
+        pad_pre[where, :] = pre
+
+    for starts in inner:
+        for row, value in rows_of_pairs(pair_conv(x3_stem, wp_first, starts), starts):
+            put(row, *gate(value, grad_act[rows_of(row), :]))
 
     has_up = (r > 0).astype(F32)
     has_down = (r < n_row - 1).astype(F32)
@@ -326,38 +361,20 @@
     for copy in cot_halos:
         copy.wait()
     take_halos(0, pad_cot, x3_cot)
+    outer = (0, 32)
     side_grad = side_conv(pad_cot, wp_second_f)
-    parts = ((0, 9), (9, 8))
-    for begin, pairs in parts:
-        pair = pair_conv(x3_cot, wp_second_f, 2 * begin, pairs)
-        for p in range(pairs):
-            for k in range(2):
-                grad_act[rows_of(2 * (begin + p) + k), :] = pair[
-                    p * 128 : (p + 1) * 128, k * 128 : (k + 1) * 128
-                ]
-
+    for row, value in rows_of_pairs(pair_conv(x3_cot, wp_second_f, outer), outer):
+        grad_act[rows_of(row), :] = value
     for copy in stem_halos:
         copy.wait()
     take_halos(1, pad_stem, x3_stem)
-
+    for row, value in rows_of_pairs(pair_conv(x3_stem, wp_first, outer), outer):
+        put(row, *gate(value, grad_act[rows_of(row), :]))
     side_act, side_pre = gate(side_conv(pad_stem, wp_first), side_grad)
-    for side, (column, there) in enumerate(((7, has_left), (136, has_right))):
+    for side, (column, there) in enumerate(zip(SIDES, (has_left, 1.0, 1.0, has_right))):
         where = pl.ds(PITCH + column, 40, stride=PITCH)
         pad_act[where, :] = side_act[side * 40 : side * 40 + 40] * there
         pad_pre[where, :] = side_pre[side * 40 : side * 40 + 40] * there
-    for begin, pairs in parts:
-        pair = pair_conv(x3_stem, wp_first, 2 * begin, pairs)
-        for p in range(pairs):
-            for k in range(2):
-                row = 2 * (begin + p) + k
-                act, pre = gate(
-                    pair[p * 128 : (p + 1) * 128, k * 128 : (k + 1) * 128],
-                    grad_act[rows_of(row), :],
-                )
-                where = pl.ds((row + 1) * PITCH + 8, 128)
-                pad_act[where, :] = act
-                pad_pre[where, :] = pre
-                pre_z[row + 1] = pre.astype(BF)
 
     blank = jnp.zeros((PITCH, 128), F32)
 
@@ -371,15 +388,18 @@
         pad_act[pl.ds(34 * PITCH, PITCH), :] = blank
         pad_pre[pl.ds(34 * PITCH, PITCH), :] = blank
 
-    pre_z[1] = jnp.zeros((128, 128), BF)
-    pre_z[34] = jnp.zeros((128, 128), BF)
-
     def shift_step(row, carry):
         shifted_row(pad_act, x3_act, row)
         shifted_row(pad_pre, x3_pre, row)
         return carry
 
     lax.fori_loop(1, 35, shift_step, 0)
+
+    def keep_step(row, carry):
+        pre_z[row] = x3_pre[pl.ds(pl.multiple_of(row * 128, 128), 128), 128:256]
+        return carry
+
+    lax.fori_loop(2, 34, keep_step, 0)
 
     def tap_grad(x3, grad, group):
         total = None
@@ -440,11 +460,16 @@
             for peer in r_peers
         ]
 
+    def chunk_of(group, owner):
+        rows = CHUNK if group < 2 else 16
+        return final.at[group, owner, 0:rows]
+
     def step3(group):
+        mine = chunk_of(group, own)
         return [
             pltpu.make_async_remote_copy(
-                final.at[group, own],
-                final.at[group, own],
+                mine,
+                mine,
                 s3_send.at[group, peer],
                 s3_recv.at[group, q],
                 (r, 2 * peer + h),
@@ -453,10 +478,10 @@
             for peer in q_peers
         ]
 
-    def step4(group):
-        mine = final.at[group, pl.ds(h * nq, nq)]
+    def step4(group, k):
+        theirs = chunk_of(group, h * nq + k)
         return pltpu.make_async_remote_copy(
-            mine, mine, s4_send.at[group], s4_recv.at[group], (r, sibling), MESH
+            theirs, theirs, s4_send.at[group, k], s4_recv.at[group, k], (r, sibling), MESH
         )
 
     def await_slots(land, sem, slots, where):
@@ -513,7 +538,6 @@
                 + land2[group, down, 0:16].astype(F32) * has_down
             )
             final[group, own, 0:16] = owned.astype(BF)
-            final[group, own, 16:80] = jnp.zeros((64, 128), BF)
         for copy in sends:
             copy.wait_send()
         sends = step3(group)
@@ -521,19 +545,29 @@
         return sends
 
     def end_step3(group, sends):
-        await_slots(final.at[group], s3_recv.at[group], q_peers, lambda s: h * nq + s)
+        passed = [step4(group, q)]
+        passed[0].start()
+        for peer in reversed(q_peers):
+            landed = chunk_of(group, h * nq + peer)
+            pltpu.make_async_remote_copy(
+                landed, landed, s3_send.at[group, peer], s3_recv.at[group, peer],
+                (r, sibling), MESH,
+            ).wait_recv()
+            copy = step4(group, peer)
+            copy.start()
+            passed.append(copy)
         for copy in sends:
             copy.wait_send()
-        copy = step4(group)
-        copy.start()
-        return copy
-
-    def end_step4(group, copy):
-        copy.wait_send()
-        theirs = final.at[group, pl.ds((1 - h) * nq, nq)]
-        pltpu.make_async_remote_copy(
-            theirs, theirs, s4_send.at[group], s4_recv.at[group], (r, sibling), MESH
-        ).wait_recv()
+        return passed
+
+    def end_step4(group, passed):
+        for copy in passed:
+            copy.wait_send()
+        for k in range(nq):
+            landed = chunk_of(group, (1 - h) * nq + k)
+            pltpu.make_async_remote_copy(
+                landed, landed, s4_send.at[group, k], s4_recv.at[group, k], (r, sibling), MESH
+            ).wait_recv()
 
     tap_grad(x3_act, cot_z, 0)
     pend_a = step0(0)
@@ -544,14 +578,14 @@
     pend_b.start()
 
     for part in range(2):
-        pair = pair_conv(x3_pre, wp_first_f, 1 + 16 * part, 8)
+        starts = tuple(range(1 + 16 * part, 17 + 16 * part, 2))
+        pair = pair_conv(x3_pre, wp_first_f, starts)
         for p in range(8):
             for k in range(2):
                 row = 16 * part + 2 * p + k
                 grad_fine[row] = (
                     pair[p * 128 : (p + 1) * 128, k * 128 : (k + 1) * 128] + cot_rows(row + 2)
                 ).astype(BF)
-    pend_a = end_step1(0, pend_a)
     pend_b = end_step0(1, pend_b)
 
     moment = jnp.zeros((512, 128), F32)
@@ -586,11 +620,11 @@
         local[2, owner * CHUNK + 48 : owner * CHUNK + 80] = lift_part
     pend_c = step0(2)
     pend_c.start()
-    pend_a = end_step2(0, pend_a)
-    pend_b = end_step1(1, pend_b)
+    pend_a = end_step1(0, pend_a)
 
     for part in range(2):
-        pair = pair_conv(x3_act, wp_second, 1 + 16 * part, 8)
+        starts = tuple(range(1 + 16 * part, 17 + 16 * part, 2))
+        pair = pair_conv(x3_act, wp_second, starts)
         for p in range(8):
             for k in range(2):
                 row = 16 * part + 2 * p + k
@@ -600,11 +634,10 @@
                 ).astype(BF)
         if part == 0:
             pend_c = end_step0(2, pend_c)
-
-    pend_a = end_step3(0, pend_a)
+    pend_b = end_step1(1, pend_b)
+    pend_a = end_step2(0, pend_a)
+    pend_c = end_step1(2, pend_c)
     pend_b = end_step2(1, pend_b)
-    pend_c = end_step1(2, pend_c)
-    end_step4(0, pend_a)
 
     def widen(group, target):
         for a in range(3):
@@ -616,12 +649,14 @@
                         group, owner, at : at + 16
                     ].astype(F32)
 
+    pend_a = end_step3(0, pend_a)
+    pend_c = end_step2(2, pend_c)
+    pend_b = end_step3(1, pend_b)
+    end_step4(0, pend_a)
     widen(0, grad_second)
-    pend_b = end_step3(1, pend_b)
-    pend_c = end_step2(2, pend_c)
+    pend_c = end_step3(2, pend_c)
     end_step4(1, pend_b)
     widen(1, grad_first)
-    pend_c = end_step3(2, pend_c)
     end_step4(2, pend_c)
     for n in range(8):
         for side in range(2):
@@ -683,14 +718,14 @@
         vm((3, nq, CHUNK, 128)),
         vm((3, n_row, CHUNK, 128)),
         vm((3, n_col, CHUNK, 128)),
-        dma((7,)),
+        dma((10,)),
         dma((2,)), dma((2,)),
         dma((2, 8)), dma((2, 8)),
         dma((3,)), dma((3,)),
         dma((3, nq)), dma((3, nq)),
         dma((3, n_row)), dma((3, n_row)),
         dma((3, nq)), dma((3, nq)),
-        dma((3,)), dma((3,)),
+        dma((3, nq)), dma((3, nq)),
     ]
     def handed(shape, dtype):
         return pltpu.VMEM(shape, dtype)

time: 66.8 us -> 57.5 us (0.86)
  Pallas kernels: 65.9 us -> 56.5 us
    pallas_call x1, Pallas kernels: 63.9 us -> 54.6 us  [body(): pl.pallas_call(functools.partial(kernel, n_row, n_col), out_shape=shapes,...]
where the time goes in v3:
time: 57.5 us; the launch traced here: 57.3 us
  Pallas kernels  56.5 us (98%)
  between operations  0.8 us (1%)
    pallas_call x1, Pallas kernels, body(): pl.pallas_call(functools.partial(kernel, n_row, n_col), out_shape=shapes,...  54.6 us
    pallas_call x1, Pallas kernels, body(): pl.pallas_call(hand_over, out_shape=tuple((jax.ShapeDtypeStruct(x.shape,...  1.96 us

profile of v3, /device:TPU:1, one launch (start us, length us, event | category | flops | bytes accessed | tf_op | source)
XLA Modules:
  0.0 57.3 jit_solution(2546117577589320500)
XLA Ops:
  0.6 54.6 %step.1 = (bf16[32,128,128]{2,1,0:T(8,128)(2,1)S(1)}, bf16[32,128,128]{2,1,0:T(8,128)(2,1)S(1)}, f32[8,32,128]{2,1,0:T(8,128)S(1)}, f32[3,3,128,128]{3,2,1,0:T(8...) custom-call(bf16[32,128,128]{2,1,0:T(8,128)(2,1)} %fine.1, bf16[8,32,128]{2,1,0:T(8,128)(2,1)} %coarse.1, ...), custom_call_target="tpu_custom_call" | custom-call | tf_op jit(solution)/shard_map/step/pallas_call | solution.py:741
  55.2 2.0 %hand_over.1 = (bf16[32,128,128]{2,1,0:T(8,128)(2,1)}, bf16[32,128,128]{2,1,0:T(8,128)(2,1)}, f32[8,32,128]{2,1,0:T(8,128)}, f32[3,3,128,128]{3,2,1,0:T(8,128)},...) custom-call(bf16[32,128,128]{2,1,0:T(8,128)(2,1)S(1)} %get-tuple-element.12.refs_0_, ...), custom_call_target="tpu_custom_call" | custom-call | tf_op jit(solution)/shard_map/hand_over/pallas_call | solution.py:755

commit v4 on v3

--- a/solution.py
+++ b/solution.py
@@ -12,6 +12,7 @@
 F32 = jnp.float32
 PITCH = 144
 CHUNK = 80
+SIZES = (CHUNK, CHUNK, 64)
 
 
 def rows_of(row, count=1, pitch=128):
@@ -127,6 +128,11 @@
     s3_recv,
     s4_send,
     s4_recv,
+    blocks_send,
+    blocks_recv,
+    lift_send,
+    lift_recv,
+    lift_sum,
 ):
     r = lax.axis_index("row")
     c = lax.axis_index("col")
@@ -284,33 +290,37 @@
         picked, lift_v[...], (((0,), (0,)), ((), ())), preferred_element_type=F32
     ).astype(BF)
 
-    def stem_step(i, carry):
+    def stem_part(part):
         lifted = lax.dot_general(
-            weights_it[:, pl.ds(pl.multiple_of(i * 512, 512), 512)],
+            weights_it[:, part * 1024 : part * 1024 + 1024],
             mix[...],
             (((0,), (0,)), ((), ())),
             preferred_element_type=F32,
-        ).reshape(4, 128, 128)
-        stem = (fine_v[pl.ds(i * 4, 4)].astype(F32) + lifted).astype(BF)
-        stem_v[pl.ds(i * 4, 4)] = stem
-        for k in range(4):
-            row = i * 4 + k + 2
-            pad_stem[pl.ds(pl.multiple_of(row * PITCH, 16) + 8, 128), :] = stem[k].astype(F32)
-            shifted_row(pad_stem, x3_stem, row)
-        return carry
-
-    stem_step(0, 0)
-    stem_step(7, 0)
+        ).reshape(8, 128, 128)
+        stem = (fine_v[part * 8 : part * 8 + 8].astype(F32) + lifted).astype(BF)
+        stem_v[part * 8 : part * 8 + 8] = stem
+        for k in range(8):
+            pad_stem[pl.ds((part * 8 + k + 2) * PITCH + 8, 128), :] = stem[k].astype(F32)
+
+    stem_part(0)
+    stem_part(3)
     stem_halos = row_halos(1, stem_v)
     for copy in stem_halos:
         copy.start()
-    lax.fori_loop(1, 7, stem_step, 0)
+    stem_part(1)
+    stem_part(2)
     fill_edges(pad_stem, 1)
     stem_sides = column_halos(1)
     for copy in stem_sides:
         copy.start()
     stem_halos = stem_halos + stem_sides
 
+    def stem_shift(row, carry):
+        shifted_row(pad_stem, x3_stem, row)
+        return carry
+
+    lax.fori_loop(2, 34, stem_shift, 0, unroll=2)
+
     def put(row, act, pre):
         where = pl.ds((row + 1) * PITCH + 8, 128)
         pad_act[where, :] = act
@@ -319,6 +329,18 @@
     for starts in inner:
         for row, value in rows_of_pairs(pair_conv(x3_stem, wp_first, starts), starts):
             put(row, *gate(value, grad_act[rows_of(row), :]))
+
+    def keep(row, begin, size):
+        where = pl.multiple_of(row * 128 + begin, 16)
+        pre_z[row, begin : begin + size] = x3_pre[pl.ds(where, size), 128:256]
+
+    def shift_step(row, carry):
+        shifted_row(pad_act, x3_act, row)
+        shifted_row(pad_pre, x3_pre, row)
+        keep(row, 0, 128)
+        return carry
+
+    lax.fori_loop(3, 33, shift_step, 0, unroll=2)
 
     has_up = (r > 0).astype(F32)
     has_down = (r < n_row - 1).astype(F32)
@@ -388,18 +410,26 @@
         pad_act[pl.ds(34 * PITCH, PITCH), :] = blank
         pad_pre[pl.ds(34 * PITCH, PITCH), :] = blank
 
-    def shift_step(row, carry):
+    for row in (1, 2, 33, 34):
         shifted_row(pad_act, x3_act, row)
         shifted_row(pad_pre, x3_pre, row)
+    keep(2, 0, 128)
+    keep(33, 0, 128)
+
+    def mend_step(row, carry):
+        base = row * 128
+        start = row * PITCH + 8
+        for pad, x3 in ((pad_act, x3_act), (pad_pre, x3_pre)):
+            for x in (0, 112):
+                for e in range(3):
+                    x3[pl.ds(pl.multiple_of(base + x, 16), 16), e * 128 : (e + 1) * 128] = pad[
+                        pl.ds(start + x + e - 1, 16), :
+                    ].astype(BF)
+        keep(row, 0, 16)
+        keep(row, 112, 16)
         return carry
 
-    lax.fori_loop(1, 35, shift_step, 0)
-
-    def keep_step(row, carry):
-        pre_z[row] = x3_pre[pl.ds(pl.multiple_of(row * 128, 128), 128), 128:256]
-        return carry
-
-    lax.fori_loop(2, 34, keep_step, 0)
+    lax.fori_loop(3, 33, mend_step, 0, unroll=2)
 
     def tap_grad(x3, grad, group):
         total = None
@@ -422,23 +452,28 @@
         for a in range(3):
             local[group, a * 384 : (a + 1) * 384] = taps[:, a * 128 : (a + 1) * 128].astype(BF)
 
-    half_rows = nq * CHUNK
 
     def step0(group):
-        return pltpu.make_async_remote_copy(
-            local.at[group, pl.ds(pl.multiple_of((1 - h) * half_rows, 16), half_rows)],
-            land0.at[group],
-            s0_send.at[group],
-            s0_recv.at[group],
-            (r, sibling),
-            MESH,
-        )
+        rows = nq * SIZES[group] // 4
+        return [
+            pltpu.make_async_remote_copy(
+                local.at[
+                    group, pl.ds(pl.multiple_of((1 - h) * 4 * rows + k * rows, 16), rows)
+                ],
+                land0.at[group, k * rows : (k + 1) * rows],
+                s0_send.at[group, k],
+                s0_recv.at[group, k],
+                (r, sibling),
+                MESH,
+            )
+            for k in range(4)
+        ]
 
     def step1(group):
         return [
             pltpu.make_async_remote_copy(
-                half.at[group, peer],
-                land1.at[group, q],
+                half.at[group, peer, 0 : SIZES[group]],
+                land1.at[group, q, 0 : SIZES[group]],
                 s1_send.at[group, peer],
                 s1_recv.at[group, q],
                 (r, 2 * peer + h),
@@ -448,17 +483,27 @@
         ]
 
     def step2(group):
-        return [
+        mine = land2.at[group, r] if group < 2 else land2.at[group, r, 48:64]
+        sends = [
             pltpu.make_async_remote_copy(
-                land2.at[group, r],
-                land2.at[group, r],
-                s2_send.at[group, peer],
-                s2_recv.at[group, r],
-                (peer, c),
-                MESH,
+                mine, mine, s2_send.at[group, peer], s2_recv.at[group, r], (peer, c), MESH
             )
             for peer in r_peers
         ]
+        if group < 2:
+            return sends
+        blocks = [
+            pltpu.make_async_remote_copy(
+                land2.at[group, r, low : low + 16],
+                land2.at[group, r, low : low + 16],
+                blocks_send.at[k],
+                blocks_recv.at[k],
+                (to, c),
+                MESH,
+            )
+            for k, (low, to) in enumerate(((0, up), (32, down)))
+        ]
+        return blocks + sends
 
     def chunk_of(group, owner):
         rows = CHUNK if group < 2 else 16
@@ -484,65 +529,78 @@
             theirs, theirs, s4_send.at[group, k], s4_recv.at[group, k], (r, sibling), MESH
         )
 
-    def await_slots(land, sem, slots, where):
-        for slot in slots:
-            pltpu.make_async_remote_copy(
-                land.at[where(slot)], land.at[where(slot)], sem.at[slot], sem.at[slot],
-                (r, sibling), MESH,
-            ).wait_recv()
+    def await_copy(landed, sem):
+        pltpu.make_async_remote_copy(landed, landed, sem, sem, (r, sibling), MESH).wait_recv()
 
     def start_all(copies):
         for copy in copies:
             copy.start()
 
-    def end_step0(group, copy):
-        copy.wait()
-        for k in range(nq):
+    def end_step0(group, copies):
+        for copy in copies:
+            copy.wait()
+        size = SIZES[group]
+        sends = step1(group)
+        for k, peer in enumerate(q_peers + [q]):
             mine = local[
-                group, pl.ds(pl.multiple_of(h * half_rows + k * CHUNK, 16), CHUNK)
+                group, pl.ds(pl.multiple_of((h * nq + peer) * size, 16), size)
             ].astype(F32)
-            theirs = land0[group, k * CHUNK : (k + 1) * CHUNK].astype(F32)
-            half[group, k] = (mine + theirs).astype(BF)
-        sends = step1(group)
-        start_all(sends)
+            theirs = land0[group, pl.ds(pl.multiple_of(peer * size, 16), size)].astype(F32)
+            half[group, peer, 0:size] = (mine + theirs).astype(BF)
+            if k < nq - 1:
+                sends[k].start()
         return sends
 
     def end_step1(group, sends):
-        await_slots(land1.at[group], s1_recv.at[group], q_peers, lambda s: s)
-        land1[group, q] = half[group, q]
-        total = land1[group, 0].astype(F32)
+        size = SIZES[group]
+        for peer in q_peers:
+            await_copy(land1.at[group, peer, 0:size], s1_recv.at[group, peer])
+        land1[group, q, 0:size] = half[group, q, 0:size]
+        total = land1[group, 0, 0:size].astype(F32)
         for k in range(1, nq):
-            total = total + land1[group, k].astype(F32)
-        land2[group, r] = total.astype(BF)
+            total = total + land1[group, k, 0:size].astype(F32)
+        land2[group, r, 0:size] = total.astype(BF)
+        following = step2(group)
+        start_all(following)
         for copy in sends:
             copy.wait_send()
-        sends = step2(group)
-        start_all(sends)
-        return sends
+        return following
 
     def end_step2(group, sends):
-        await_slots(land2.at[group], s2_recv.at[group], r_peers, lambda s: s)
         if group < 2:
+            for peer in r_peers:
+                await_copy(land2.at[group, peer], s2_recv.at[group, peer])
             total = land2[group, 0].astype(F32)
             for k in range(1, n_row):
                 total = total + land2[group, k].astype(F32)
             final[group, own] = (total * (1.0 / 1024.0)).astype(BF)
         else:
-            total = land2[group, 0, 48:80].astype(F32)
-            for k in range(1, n_row):
-                total = total + land2[group, k, 48:80].astype(F32)
-            grad_lift[...] = total * (1.0 / 1024.0)
+            await_copy(land2.at[group, up, 32:48], blocks_recv.at[1])
+            await_copy(land2.at[group, down, 0:16], blocks_recv.at[0])
             owned = (
                 land2[group, r, 16:32].astype(F32)
                 + land2[group, up, 32:48].astype(F32) * has_up
                 + land2[group, down, 0:16].astype(F32) * has_down
             )
             final[group, own, 0:16] = owned.astype(BF)
+        following = step3(group)
+        start_all(following)
         for copy in sends:
             copy.wait_send()
-        sends = step3(group)
-        start_all(sends)
-        return sends
+        return following
+
+    def lift_step2():
+        for peer in r_peers:
+            await_copy(land2.at[2, peer, 48:64], s2_recv.at[2, peer])
+        total = land2[2, 0, 48:64].astype(F32)
+        for k in range(1, n_row):
+            total = total + land2[2, k, 48:64].astype(F32)
+        lift_sum[h] = (total * (1.0 / 1024.0)).astype(BF)
+        copy = pltpu.make_async_remote_copy(
+            lift_sum.at[h], lift_sum.at[h], lift_send, lift_recv, (r, sibling), MESH
+        )
+        copy.start()
+        return copy
 
     def end_step3(group, sends):
         passed = [step4(group, q)]
@@ -571,11 +629,11 @@
 
     tap_grad(x3_act, cot_z, 0)
     pend_a = step0(0)
-    pend_a.start()
+    start_all(pend_a)
     tap_grad(x3_stem, pre_z, 1)
     pend_a = end_step0(0, pend_a)
     pend_b = step0(1)
-    pend_b.start()
+    start_all(pend_b)
 
     for part in range(2):
         starts = tuple(range(1 + 16 * part, 17 + 16 * part, 2))
@@ -595,15 +653,11 @@
             grad_fine[part * 8 : part * 8 + 8].reshape(1024, 128),
             preferred_element_type=F32,
         )
-    high = moment.astype(BF)
-    rest = (moment - high.astype(F32)).astype(BF)
-    lift_part = jnp.dot(picked, high, preferred_element_type=F32) + jnp.dot(
-        picked, rest, preferred_element_type=F32
+    moment = moment.astype(BF)
+    lift_part = jnp.dot(picked, moment, preferred_element_type=F32)
+    blocks = lax.dot_general(
+        lift_v[...], moment, (((1,), (1,)), ((), ())), preferred_element_type=F32
     )
-    across = (((1,), (1,)), ((), ()))
-    blocks = lax.dot_general(
-        lift_v[...], high, across, preferred_element_type=F32
-    ) + lax.dot_general(lift_v[...], rest, across, preferred_element_type=F32)
     lift_part = lift_part.astype(BF)
     for section in range(3):
         for n in range(8):
@@ -614,27 +668,25 @@
                 )
             value = value.astype(BF)
             for side in range(2):
-                low = (2 * n + side) * CHUNK + section * 16
+                low = (2 * n + side) * SIZES[2] + section * 16
                 local[2, low : low + 16] = value[side * 16 : side * 16 + 16]
     for owner in range(n_col):
-        local[2, owner * CHUNK + 48 : owner * CHUNK + 80] = lift_part
+        low = owner * SIZES[2] + 48
+        part = owner // nq * 16
+        local[2, low : low + 16] = lift_part[part : part + 16]
     pend_c = step0(2)
-    pend_c.start()
+    start_all(pend_c)
     pend_a = end_step1(0, pend_a)
 
-    for part in range(2):
+    def output_part(part):
         starts = tuple(range(1 + 16 * part, 17 + 16 * part, 2))
-        pair = pair_conv(x3_act, wp_second, starts)
-        for p in range(8):
-            for k in range(2):
-                row = 16 * part + 2 * p + k
-                out[row] = (
-                    pair[p * 128 : (p + 1) * 128, k * 128 : (k + 1) * 128]
-                    + stem_v[row].astype(F32)
-                ).astype(BF)
-        if part == 0:
-            pend_c = end_step0(2, pend_c)
+        for row, value in rows_of_pairs(pair_conv(x3_act, wp_second, starts), starts):
+            out[row - 1] = (value + stem_v[row - 1].astype(F32)).astype(BF)
+
+    output_part(0)
+    pend_c = end_step0(2, pend_c)
     pend_b = end_step1(1, pend_b)
+    output_part(1)
     pend_a = end_step2(0, pend_a)
     pend_c = end_step1(2, pend_c)
     pend_b = end_step2(1, pend_b)
@@ -649,12 +701,17 @@
                         group, owner, at : at + 16
                     ].astype(F32)
 
+    pend_c = end_step2(2, pend_c)
     pend_a = end_step3(0, pend_a)
-    pend_c = end_step2(2, pend_c)
-    pend_b = end_step3(1, pend_b)
+    lift_copy = lift_step2()
     end_step4(0, pend_a)
     widen(0, grad_second)
+    pend_b = end_step3(1, pend_b)
     pend_c = end_step3(2, pend_c)
+    lift_copy.wait_send()
+    await_copy(lift_sum.at[1 - h], lift_recv)
+    for part in range(2):
+        grad_lift[part * 16 : part * 16 + 16] = lift_sum[part].astype(F32)
     end_step4(1, pend_b)
     widen(1, grad_first)
     end_step4(2, pend_c)
@@ -721,11 +778,13 @@
         dma((10,)),
         dma((2,)), dma((2,)),
         dma((2, 8)), dma((2, 8)),
-        dma((3,)), dma((3,)),
+        dma((3, 4)), dma((3, 4)),
         dma((3, nq)), dma((3, nq)),
         dma((3, n_row)), dma((3, n_row)),
         dma((3, nq)), dma((3, nq)),
         dma((3, nq)), dma((3, nq)),
+        dma((2,)), dma((2,)), dma, dma,
+        vm((2, 16, 128)),
     ]
     def handed(shape, dtype):
         return pltpu.VMEM(shape, dtype)

time: 57.5 us -> 54.9 us (0.955)
  Pallas kernels: 56.5 us -> 54 us
    pallas_call x1, Pallas kernels: 54.6 us -> 52 us  [body(): pl.pallas_call(functools.partial(kernel, n_row, n_col), out_shape=shapes,...]
where the time goes in v4:
time: 54.9 us; the launch traced here: 54.8 us
  Pallas kernels  54 us (98%)
  between operations  0.8 us (1%)
    pallas_call x1, Pallas kernels, body(): pl.pallas_call(functools.partial(kernel, n_row, n_col), out_shape=shapes,...  52 us
    pallas_call x1, Pallas kernels, body(): pl.pallas_call(hand_over, out_shape=tuple((jax.ShapeDtypeStruct(x.shape,...  1.96 us

profile of v4, /device:TPU:1, one launch (start us, length us, event | category | flops | bytes accessed | tf_op | source)
XLA Modules:
  0.0 54.8 jit_solution(13416200438751778471)
XLA Ops:
  0.6 52.0 %step.1 = (bf16[32,128,128]{2,1,0:T(8,128)(2,1)S(1)}, bf16[32,128,128]{2,1,0:T(8,128)(2,1)S(1)}, f32[8,32,128]{2,1,0:T(8,128)S(1)}, f32[3,3,128,128]{3,2,1,0:T(8...) custom-call(bf16[32,128,128]{2,1,0:T(8,128)(2,1)} %fine.1, bf16[8,32,128]{2,1,0:T(8,128)(2,1)} %coarse.1, ...), custom_call_target="tpu_custom_call" | custom-call | tf_op jit(solution)/shard_map/step/pallas_call | solution.py:800
  52.6 2.0 %hand_over.1 = (bf16[32,128,128]{2,1,0:T(8,128)(2,1)}, bf16[32,128,128]{2,1,0:T(8,128)(2,1)}, f32[8,32,128]{2,1,0:T(8,128)}, f32[3,3,128,128]{3,2,1,0:T(8,128)},...) custom-call(bf16[32,128,128]{2,1,0:T(8,128)(2,1)S(1)} %get-tuple-element.12.refs_0_, ...), custom_call_target="tpu_custom_call" | custom-call | tf_op jit(solution)/shard_map/hand_over/pallas_call | solution.py:814

commit v5 on v4

--- a/solution.py
+++ b/solution.py
@@ -105,6 +105,7 @@
     edge_send,
     land_row,
     land_col,
+    corner_send,
     land_corner,
     taps,
     local,
@@ -197,10 +198,10 @@
         return [
             halo_copy(which, 2, edges.at[0], land_col.at[which, 1], (r, left)),
             halo_copy(which, 3, edges.at[1], land_col.at[which, 0], (r, right)),
-            halo_copy(which, 4, edges.at[0, :, 0:16], land_corner.at[which, 3], (up, left)),
-            halo_copy(which, 5, edges.at[1, :, 0:16], land_corner.at[which, 2], (up, right)),
-            halo_copy(which, 6, edges.at[0, :, 16:32], land_corner.at[which, 1], (down, left)),
-            halo_copy(which, 7, edges.at[1, :, 16:32], land_corner.at[which, 0], (down, right)),
+            halo_copy(which, 4, corner_send.at[which, 0], land_corner.at[which, 3], (up, left)),
+            halo_copy(which, 5, corner_send.at[which, 1], land_corner.at[which, 2], (up, right)),
+            halo_copy(which, 6, corner_send.at[which, 2], land_corner.at[which, 1], (down, left)),
+            halo_copy(which, 7, corner_send.at[which, 3], land_corner.at[which, 0], (down, right)),
         ]
 
     pl.semaphore_wait(barrier, len(peers))
@@ -235,7 +236,19 @@
                     pl.ds(2 * PITCH + 8 + x, 32, stride=PITCH), :
                 ].astype(BF)
 
+    def fill_corners(pad, which):
+        for corner in range(4):
+            low, side = divmod(corner, 2)
+            cells = [
+                pad[pl.ds(((32 if low else 2) + k) * PITCH + 8 + (126 if side else 0) + j, 1), :]
+                for j in range(2)
+                for k in range(2)
+            ]
+            cells.append(jnp.zeros((12, 128), F32))
+            corner_send[which, corner] = jnp.concatenate(cells, 0).astype(BF)
+
     fill_edges(pad_cot, 0)
+    fill_corners(pad_cot, 0)
     cot_sides = column_halos(0)
     for copy in cot_sides:
         copy.start()
@@ -310,6 +323,7 @@
     stem_part(1)
     stem_part(2)
     fill_edges(pad_stem, 1)
+    fill_corners(pad_stem, 1)
     stem_sides = column_halos(1)
     for copy in stem_sides:
         copy.start()
@@ -361,10 +375,10 @@
         for corner in range(4):
             low, side = divmod(corner, 2)
             there = (has_up, has_down)[low] * (has_left, has_right)[side]
+            tile = land_corner[which, corner].astype(F32) * there
             for j in range(2):
-                tile = land_corner[which, corner, j].astype(F32) * there
                 for k in range(2):
-                    source = k if low else 14 + k
+                    source = 2 * j + k
                     row = 34 + k if low else k
                     column = (6, 136)[side] + j
                     pad[pl.ds(row * PITCH + column, 1), :] = tile[source : source + 1]
@@ -523,11 +537,19 @@
             for peer in q_peers
         ]
 
-    def step4(group, k):
-        theirs = chunk_of(group, h * nq + k)
-        return pltpu.make_async_remote_copy(
-            theirs, theirs, s4_send.at[group, k], s4_recv.at[group, k], (r, sibling), MESH
-        )
+    def quarters(group, core):
+        if group == 2:
+            return [final.at[2, pl.ds(core * nq, nq), 0:16]]
+        size = nq // 4
+        return [final.at[group, pl.ds(core * nq + k * size, size)] for k in range(4)]
+
+    def step4(group):
+        return [
+            pltpu.make_async_remote_copy(
+                piece, piece, s4_send.at[group, k], s4_recv.at[group, k], (r, sibling), MESH
+            )
+            for k, piece in enumerate(quarters(group, h))
+        ]
 
     def await_copy(landed, sem):
         pltpu.make_async_remote_copy(landed, landed, sem, sem, (r, sibling), MESH).wait_recv()
@@ -603,17 +625,10 @@
         return copy
 
     def end_step3(group, sends):
-        passed = [step4(group, q)]
-        passed[0].start()
-        for peer in reversed(q_peers):
-            landed = chunk_of(group, h * nq + peer)
-            pltpu.make_async_remote_copy(
-                landed, landed, s3_send.at[group, peer], s3_recv.at[group, peer],
-                (r, sibling), MESH,
-            ).wait_recv()
-            copy = step4(group, peer)
-            copy.start()
-            passed.append(copy)
+        for peer in q_peers:
+            await_copy(chunk_of(group, h * nq + peer), s3_recv.at[group, peer])
+        passed = step4(group)
+        start_all(passed)
         for copy in sends:
             copy.wait_send()
         return passed
@@ -621,11 +636,8 @@
     def end_step4(group, passed):
         for copy in passed:
             copy.wait_send()
-        for k in range(nq):
-            landed = chunk_of(group, (1 - h) * nq + k)
-            pltpu.make_async_remote_copy(
-                landed, landed, s4_send.at[group, k], s4_recv.at[group, k], (r, sibling), MESH
-            ).wait_recv()
+        for k, piece in enumerate(quarters(group, 1 - h)):
+            await_copy(piece, s4_recv.at[group, k])
 
     tap_grad(x3_act, cot_z, 0)
     pend_a = step0(0)
@@ -704,10 +716,10 @@
     pend_c = end_step2(2, pend_c)
     pend_a = end_step3(0, pend_a)
     lift_copy = lift_step2()
+    pend_b = end_step3(1, pend_b)
+    pend_c = end_step3(2, pend_c)
     end_step4(0, pend_a)
     widen(0, grad_second)
-    pend_b = end_step3(1, pend_b)
-    pend_c = end_step3(2, pend_c)
     lift_copy.wait_send()
     await_copy(lift_sum.at[1 - h], lift_recv)
     for part in range(2):
@@ -725,7 +737,7 @@
     copies = []
     for k in range(6):
         source, target = refs[k], refs[6 + k]
-        pieces = 4 if k < 2 else 1
+        pieces = (4, 4, 1, 3, 3, 1)[k]
         size = source.shape[0] // pieces
         for p in range(pieces):
             part = pl.ds(p * size, size)
@@ -767,7 +779,8 @@
         vm((2, 2, 2, 32, 128)),
         vm((2, 2, 2, 128, 128)),
         vm((2, 2, 2, 32, 128)),
-        vm((2, 4, 2, 16, 128)),
+        vm((2, 4, 16, 128)),
+        vm((2, 4, 16, 128)),
         vm((384, 384), F32),
         vm((3, n_col * CHUNK, 128)),
         vm((3, nq * CHUNK, 128)),

time: 54.9 us -> 54.8 us (level)
  no operation moved by 1% of the time
where the time goes in v5:
time: 54.8 us; the launch traced here: 54.7 us
  Pallas kernels  53.9 us (98%)
  between operations  0.8 us (1%)
    pallas_call x1, Pallas kernels, body(): pl.pallas_call(functools.partial(kernel, n_row, n_col), out_shape=shapes,...  52 us
    pallas_call x1, Pallas kernels, body(): pl.pallas_call(hand_over, out_shape=tuple((jax.ShapeDtypeStruct(x.shape,...  1.95 us

profile of v5, /device:TPU:1, one launch (start us, length us, event | category | flops | bytes accessed | tf_op | source)
XLA Modules:
  0.0 54.7 jit_solution(6000155962406866305)
XLA Ops:
  0.6 52.0 %step.1 = (bf16[32,128,128]{2,1,0:T(8,128)(2,1)S(1)}, bf16[32,128,128]{2,1,0:T(8,128)(2,1)S(1)}, f32[8,32,128]{2,1,0:T(8,128)S(1)}, f32[3,3,128,128]{3,2,1,0:T(8...) custom-call(bf16[32,128,128]{2,1,0:T(8,128)(2,1)} %fine.1, bf16[8,32,128]{2,1,0:T(8,128)(2,1)} %coarse.1, ...), custom_call_target="tpu_custom_call" | custom-call | tf_op jit(solution)/shard_map/step/pallas_call | solution.py:813
  52.6 1.9 %hand_over.1 = (bf16[32,128,128]{2,1,0:T(8,128)(2,1)}, bf16[32,128,128]{2,1,0:T(8,128)(2,1)}, f32[8,32,128]{2,1,0:T(8,128)}, f32[3,3,128,128]{3,2,1,0:T(8,128)},...) custom-call(bf16[32,128,128]{2,1,0:T(8,128)(2,1)S(1)} %get-tuple-element.12.refs_0_, ...), custom_call_target="tpu_custom_call" | custom-call | tf_op jit(solution)/shard_map/hand_over/pallas_call | solution.py:827
